TPU v7x, 32 devices: a whole 2x2x4 slice. The times are simulated.
32 devices in a mesh: grp: 4 (over y, core), fsdp: 8 (over z, x).
Axes of the slice: x: 2, y: 2, z: 4, core: 2. Of those that a mesh axis runs over, the one named last changes fastest.
Arguments:
- patches: bfloat16 [128, 196, 768], P(('grp', 'fsdp')), may hold values from -6 to 6
- positions: int32 [128, 75], P(('grp', 'fsdp')), may hold values from 1 to 196, as said below
- codes: int32 [128, 75], P(('grp', 'fsdp')), may hold values from 0 to 8191
- owners: int32 [8], replicated, may hold values from 0 to 3
- bases: float32 [8, 768, 768], replicated, as said below
- patch_weight: float32 [768, 768], P(None, 'fsdp'), may hold values from -0.21875 to 0.21875
- head_weight: float32 [768, 8192], P(None, 'fsdp'), may hold values from -0.21875 to 0.21875
- vocab_bias: float32 [8192], P('fsdp'), may hold values from -3 to 3
- token_vectors: float32 [5, 768], replicated
- qkv_weight: float32 [2, 768, 2304], P(None, None, 'fsdp'), may hold values from -0.21875 to 0.21875
- out_weight: float32 [2, 768, 768], P(None, None, 'fsdp'), may hold values from -0.625 to 0.625
- up_weight: float32 [2, 768, 3072], P(None, None, 'fsdp'), may hold values from -0.21875 to 0.21875
- down_weight: float32 [2, 3072, 768], P(None, 'fsdp'), may hold values from -0.109375 to 0.109375
- layer_vectors: float32 [2, 19536], replicated
- first_patch: float32 [768, 768], P(None, 'fsdp'), may hold values from -0.00012207031 to 0.00012207031
- first_head: float32 [768, 8192], P(None, 'fsdp'), may hold values from -0.00012207031 to 0.00012207031
- first_vocab: float32 [8192], P('fsdp'), may hold values from -0.00061035156 to 0.00061035156
- first_token: float32 [5, 768], replicated, may hold values from -0.00061035156 to 0.00061035156
- first_qkv: float32 [2, 768, 2304], P(None, None, 'fsdp'), may hold values from -0.00012207031 to 0.00012207031
- first_out: float32 [2, 768, 768], P(None, None, 'fsdp'), may hold values from -0.00012207031 to 0.00012207031
- first_up: float32 [2, 768, 3072], P(None, None, 'fsdp'), may hold values from -0.00012207031 to 0.00012207031
- first_down: float32 [2, 3072, 768], P(None, 'fsdp'), may hold values from -0.00012207031 to 0.00012207031
- first_layer: float32 [2, 19536], replicated, may hold values from -0.00061035156 to 0.00061035156
- second_patch: float32 [768, 768], P(None, 'fsdp'), may hold values from 4.7419974e-11 to 1.896799e-10
- second_head: float32 [768, 8192], P(None, 'fsdp'), may hold values from 4.7419974e-11 to 1.896799e-10
- second_vocab: float32 [8192], P('fsdp'), may hold values from 1.1854994e-09 to 4.7419975e-09
- second_token: float32 [5, 768], replicated, may hold values from 1.1854994e-09 to 4.7419975e-09
- second_qkv: float32 [2, 768, 2304], P(None, None, 'fsdp'), may hold values from 4.7419974e-11 to 1.896799e-10
- second_out: float32 [2, 768, 768], P(None, None, 'fsdp'), may hold values from 4.7419974e-11 to 1.896799e-10
- second_up: float32 [2, 768, 3072], P(None, None, 'fsdp'), may hold values from 4.7419974e-11 to 1.896799e-10
- second_down: float32 [2, 3072, 768], P(None, 'fsdp'), may hold values from 4.7419974e-11 to 1.896799e-10
- second_layer: float32 [2, 19536], replicated, may hold values from 1.1854994e-09 to 4.7419975e-09
Outputs:
- loss_sum: float32 [], replicated
- clip_norm: float32 [], replicated
- new_patch: float32 [768, 768], P(None, 'fsdp')
- new_head: float32 [768, 8192], P(None, 'fsdp')
- new_vocab: float32 [8192], P('fsdp')
- new_token: float32 [5, 768], replicated
- new_qkv: float32 [2, 768, 2304], P(None, None, 'fsdp')
- new_out: float32 [2, 768, 768], P(None, None, 'fsdp')
- new_up: float32 [2, 768, 3072], P(None, None, 'fsdp')
- new_down: float32 [2, 3072, 768], P(None, 'fsdp')
- new_layer: float32 [2, 19536], replicated
- moment_patch: float32 [768, 768], P(None, 'fsdp')
- moment_head: float32 [768, 8192], P(None, 'fsdp')
- moment_vocab: float32 [8192], P('fsdp')
- moment_token: float32 [5, 768], replicated
- moment_qkv: float32 [2, 768, 2304], P(None, None, 'fsdp')
- moment_out: float32 [2, 768, 768], P(None, None, 'fsdp')
- moment_up: float32 [2, 768, 3072], P(None, None, 'fsdp')
- moment_down: float32 [2, 3072, 768], P(None, 'fsdp')
- moment_layer: float32 [2, 19536], replicated
- square_patch: float32 [768, 768], P(None, 'fsdp')
- square_head: float32 [768, 8192], P(None, 'fsdp')
- square_vocab: float32 [8192], P('fsdp')
- square_token: float32 [5, 768], replicated
- square_qkv: float32 [2, 768, 2304], P(None, None, 'fsdp')
- square_out: float32 [2, 768, 768], P(None, None, 'fsdp')
- square_up: float32 [2, 768, 3072], P(None, None, 'fsdp')
- square_down: float32 [2, 3072, 768], P(None, 'fsdp')
- square_layer: float32 [2, 19536], replicated
Inputs may be any that keep to these rules, and one draw needn't show every extreme that they name: The 75 positions of an image are distinct token indices of patches. `bases`: each basis is orthogonal.
All inputs are finite; a program needn't handle non-finite values.
Results may differ from a plain program's by a relative error of at most 0.018.
Values may be sent and summed in bfloat16 or wider, within the bound.
A program may use at most 448 MiB of HBM per device.

v0:
```python
import jax
import jax.numpy as jnp
import numpy as np
from jax import lax
from jax.sharding import PartitionSpec as P

D = 768
H = 12
HD = 64
FF = 3072
SIDE = 14
NMASK = 75
MICRO = 2
STEP = 10
NPATCH = 196
NREL = 732


highest = lax.Precision.HIGHEST
beta_one = 0.9
beta_two = 0.999
adam_eps = 1e-08
matrix_rate = 0.06
vector_rate = 0.5
weight_decay = 0.05
clip_level = 1.0
norm_eps = 1e-06


def combined_all(x, axis, combine):
    everything = jax.tree.map(lambda part: lax.all_gather(part, axis), x)
    leading = jax.tree.map(lambda part: part[0], everything)

    def lap(k, so_far):
        return combine(so_far, jax.tree.map(lambda part: part[k], everything))

    return lax.fori_loop(1, lax.axis_size(axis), lap, leading)


def spread_2(block, axis, source):
    block = jnp.where(lax.axis_index(axis) == source, block, jnp.zeros_like(block))
    return lax.psum(block, axis)


def round_value(value):
    return lax.optimization_barrier(value.astype(jnp.bfloat16)).astype(jnp.float32)


def same_value(value):
    return value


def round_keep(value):
    return (round_value(value), None)


def grad_pass(kept, grad):
    return (grad,)


def pass_keep(value):
    return (value, None)


def grad_round(kept, grad):
    return (round_value(grad),)


def low(value):
    wrapped = jax.custom_vjp(round_value)
    wrapped.defvjp(round_keep, grad_pass)
    return wrapped(value)


def low_back(value):
    wrapped = jax.custom_vjp(same_value)
    wrapped.defvjp(pass_keep, grad_round)
    return wrapped(value)


def product(left_side, right_side):
    return jnp.dot(left_side, right_side, precision=highest, preferred_element_type=jnp.float32)


def offset_table(side):
    span = 2 * side - 1
    first = np.arange(side)[:, None, None]
    second = np.arange(side)[None, :, None]
    slots = np.arange(span)[None, None, :]
    return jnp.asarray((first - second + side - 1 == slots).astype(np.float32))


def position_bias(bias_table):
    heads = bias_table.shape[0]
    span = 2 * SIDE - 1
    far_count = span * span
    inner = bias_table[:, :far_count].reshape(heads, span, span)
    pick = offset_table(SIDE)
    along = jnp.einsum("hrc,xwc->hrxw", inner, pick, precision=highest)
    grid = jnp.einsum("hrxw,yvr->hyxvw", along, pick, precision=highest).reshape(
        heads, NPATCH, NPATCH
    )
    corner = bias_table[:, far_count + 2 : far_count + 3]
    top = jnp.concatenate(
        [corner, jnp.broadcast_to(bias_table[:, far_count : far_count + 1], (heads, NPATCH))],
        axis=1,
    )
    left = jnp.broadcast_to(bias_table[:, far_count + 1 : far_count + 2, None], (heads, NPATCH, 1))
    rest = jnp.concatenate([left, grid], axis=2)
    return jnp.concatenate([top[:, None, :], rest], axis=1)


def layer_norm(values, gain_row, bias_row):
    centered = values - jnp.mean(values, axis=-1, keepdims=True)
    spread = jnp.mean(centered * centered, axis=-1, keepdims=True)
    return centered * lax.rsqrt(spread + norm_eps) * gain_row + bias_row


def unpack(vectors):
    pieces = [vectors[slot * D : (slot + 1) * D] for slot in range(10)]
    fc_bias = vectors[10 * D : 10 * D + FF]
    bias_table = vectors[10 * D + FF :].reshape(H, NREL)
    return (pieces, fc_bias, bias_table)


def layer(states, qkv_weight, out_weight, up_weight, down_weight, vectors):
    pieces, fc_bias, bias_table = unpack(vectors)
    (
        gain_one,
        bias_one,
        query_bias,
        value_bias,
        out_bias,
        scale_one,
        gain_two,
        bias_two,
        down_bias,
        scale_two,
    ) = pieces
    count, length = (states.shape[0], states.shape[1])
    normed = low(layer_norm(states, gain_one, bias_one))
    qkv_bias = jnp.concatenate([query_bias, jnp.zeros_like(query_bias), value_bias])
    projected = low(low_back(product(normed, low(qkv_weight)) + qkv_bias)).reshape(
        count, length, 3, H, HD
    )
    scores = low_back(
        jnp.einsum("nqhd,nkhd->nhqk", projected[:, :, 0], projected[:, :, 1], precision=highest)
    )
    scores = scores * HD ** (-0.5) + position_bias(bias_table)[None]
    attention = low(jax.nn.softmax(scores, axis=-1))
    attended = low(
        low_back(jnp.einsum("nhqk,nkhd->nqhd", attention, projected[:, :, 2], precision=highest))
    )
    attended = attended.reshape(count, length, D)
    states = states + scale_one * low_back(product(attended, low(out_weight)) + out_bias)
    normed_two = low(layer_norm(states, gain_two, bias_two))
    hidden = low(
        jax.nn.gelu(low_back(product(normed_two, low(up_weight)) + fc_bias), approximate=False)
    )
    return states + scale_two * low_back(product(hidden, low(down_weight)) + down_bias)


def patch_mask(positions):
    slots = jnp.arange(1, NPATCH + 1, dtype=jnp.int32)
    return jnp.sum((positions[:, :, None] == slots[None, None, :]).astype(jnp.float32), axis=1)


def embed(patches, patch_weight, token_vectors, masked):
    tokens = low_back(product(low(patches), low(patch_weight)) + token_vectors[0])
    tokens = tokens * (1.0 - masked[..., None]) + token_vectors[2] * masked[..., None]
    leading = jnp.broadcast_to(token_vectors[1], (tokens.shape[0], 1, D))
    return jnp.concatenate([leading, tokens], axis=1)


def final_rows(states, token_vectors, positions):
    normed = layer_norm(states, token_vectors[3], token_vectors[4])
    slots = jnp.arange(states.shape[1], dtype=jnp.int32)
    select = (positions[:, :, None] == slots[None, None, :]).astype(jnp.float32)
    return low(jnp.einsum("nms,nsd->nmd", select, normed, precision=highest))


def adam_step(weight, grad, first_moment, second_moment, decay, rate):
    first_moment = beta_one * first_moment + (1 - beta_one) * grad
    second_moment = beta_two * second_moment + (1 - beta_two) * grad * grad
    update = (
        first_moment
        / (1 - beta_one**STEP)
        / (jnp.sqrt(second_moment / (1 - beta_two**STEP)) + adam_eps)
    )
    return (weight - rate * (update + decay * weight), first_moment, second_moment)


def rotated_step(weight, grad, first_moment, second_moment, basis, on_left):
    turned = product(basis.T, grad) if on_left else product(grad, basis)
    first_moment = beta_one * first_moment + (1 - beta_one) * turned
    second_moment = beta_two * second_moment + (1 - beta_two) * turned * turned
    update = (
        first_moment
        / (1 - beta_one**STEP)
        / (jnp.sqrt(second_moment / (1 - beta_two**STEP)) + adam_eps)
    )
    update = product(basis, update) if on_left else product(update, basis.T)
    return (weight - matrix_rate * (update + weight_decay * weight), first_moment, second_moment)


def combine_stats(earlier, later):
    top = jnp.maximum(earlier[0], later[0])
    total = earlier[1] * jnp.exp(earlier[0] - top) + later[1] * jnp.exp(later[0] - top)
    return (top, total, earlier[2] + later[2])


def widen(pieces):
    return tuple((piece.astype(jnp.float32) for piece in pieces))


def body(
    patches,
    positions,
    codes,
    owners,
    bases,
    patch_weight,
    head_weight,
    vocab_bias,
    token_vectors,
    qkv_weight,
    out_weight,
    up_weight,
    down_weight,
    layer_vectors,
    first_patch,
    first_head,
    first_vocab,
    first_token,
    first_qkv,
    first_out,
    first_up,
    first_down,
    first_layer,
    second_patch,
    second_head,
    second_vocab,
    second_token,
    second_qkv,
    second_out,
    second_up,
    second_down,
    second_layer,
):
    layers = qkv_weight.shape[0]
    per_batch = patches.shape[0] // MICRO
    row_count = per_batch * NMASK
    vocab_local = head_weight.shape[1]
    vocab_start = lax.axis_index("fsdp") * vocab_local
    vocab_ids = vocab_start + jnp.arange(vocab_local, dtype=jnp.int32)
    head_low = low(head_weight)
    grad_patch = jnp.zeros_like(patch_weight)
    grad_head = jnp.zeros_like(head_weight)
    grad_vocab = jnp.zeros_like(vocab_bias)
    grad_token = jnp.zeros_like(token_vectors)
    shard_first = (qkv_weight[0], out_weight[0], up_weight[0], down_weight[0])
    grad_mats = [[jnp.zeros_like(shard) for layer_index in range(layers)] for shard in shard_first]
    layer_parts = [jnp.zeros_like(layer_vectors[0]) for layer_index in range(layers)]
    loss_sum = jnp.zeros((), jnp.float32)
    for micro_index in range(MICRO):
        lower = micro_index * per_batch
        patch_group = patches[lower : lower + per_batch].astype(jnp.float32)
        position_group = positions[lower : lower + per_batch]
        code_group = codes[lower : lower + per_batch].reshape(-1)
        masked = patch_mask(position_group)
        patch_full = lax.all_gather(
            patch_weight.astype(jnp.bfloat16), "fsdp", axis=1, tiled=True
        ).astype(jnp.float32)
        states, embed_pull = jax.vjp(
            lambda weight, vectors: embed(patch_group, weight, vectors, masked),
            patch_full,
            token_vectors,
        )
        inputs = []
        gathered = []
        for layer_index in range(layers):
            full = widen(
                (
                    lax.all_gather(
                        qkv_weight[layer_index].astype(jnp.bfloat16), "fsdp", axis=1, tiled=True
                    ),
                    lax.all_gather(
                        out_weight[layer_index].astype(jnp.bfloat16), "fsdp", axis=1, tiled=True
                    ),
                    lax.all_gather(
                        up_weight[layer_index].astype(jnp.bfloat16), "fsdp", axis=1, tiled=True
                    ),
                    lax.all_gather(
                        down_weight[layer_index].astype(jnp.bfloat16), "fsdp", axis=0, tiled=True
                    ),
                )
            )
            inputs.append(states)
            gathered.append(full)
            states = layer(states, *full, layer_vectors[layer_index])
        rows, final_pull = jax.vjp(
            lambda values, vectors: final_rows(values, vectors, position_group),
            states,
            token_vectors,
        )
        all_rows, all_codes = (
            lax.all_gather(rows.reshape(-1, D).astype(jnp.bfloat16), "fsdp", axis=0, tiled=True),
            lax.all_gather(code_group, "fsdp", axis=0, tiled=True),
        )
        all_rows = all_rows.astype(jnp.float32)
        logits = product(all_rows, head_low) + vocab_bias
        local_max = jnp.max(logits, axis=1)
        local_sum = jnp.sum(jnp.exp(logits - local_max[:, None]), axis=1)
        hits = (all_codes[:, None] == vocab_ids[None, :]).astype(jnp.float32)
        local_target = jnp.sum(hits * logits, axis=1)
        top, total, target = combined_all(
            (local_max, local_sum, local_target), "fsdp", combine_stats
        )
        log_total = top + jnp.log(total)
        row_loss = log_total - target
        loss_sum = loss_sum + jnp.sum(
            lax.dynamic_slice_in_dim(row_loss, lax.axis_index("fsdp") * row_count, row_count)
        )
        logit_grads = jnp.exp(logits - log_total[:, None]) - hits
        rounded = low(logit_grads)
        grad_head = grad_head + product(all_rows.T, rounded)
        grad_vocab = grad_vocab + jnp.sum(logit_grads, axis=0)
        row_grads = lax.psum_scatter(
            product(rounded, head_low.T), "fsdp", scatter_dimension=0, tiled=True
        )
        back, token_part = final_pull(row_grads.reshape(rows.shape))
        grad_token = grad_token + token_part
        for layer_index in reversed(range(layers)):
            full = widen(
                (
                    lax.all_gather(
                        qkv_weight[layer_index].astype(jnp.bfloat16), "fsdp", axis=1, tiled=True
                    ),
                    lax.all_gather(
                        out_weight[layer_index].astype(jnp.bfloat16), "fsdp", axis=1, tiled=True
                    ),
                    lax.all_gather(
                        up_weight[layer_index].astype(jnp.bfloat16), "fsdp", axis=1, tiled=True
                    ),
                    lax.all_gather(
                        down_weight[layer_index].astype(jnp.bfloat16), "fsdp", axis=0, tiled=True
                    ),
                )
            )
            unused, layer_pull = jax.vjp(
                layer, inputs[layer_index], *full, layer_vectors[layer_index]
            )
            back, delta_qkv, delta_out, delta_up, delta_down, delta_vectors = layer_pull(back)
            summed = (
                lax.psum_scatter(
                    delta_qkv.astype(jnp.bfloat16), "fsdp", scatter_dimension=1, tiled=True
                ).astype(jnp.float32),
                lax.psum_scatter(
                    delta_out.astype(jnp.bfloat16), "fsdp", scatter_dimension=1, tiled=True
                ).astype(jnp.float32),
                lax.psum_scatter(
                    delta_up.astype(jnp.bfloat16), "fsdp", scatter_dimension=1, tiled=True
                ).astype(jnp.float32),
                lax.psum_scatter(
                    delta_down.astype(jnp.bfloat16), "fsdp", scatter_dimension=0, tiled=True
                ).astype(jnp.float32),
            )
            for kind_index in range(4):
                grad_mats[kind_index][layer_index] = (
                    grad_mats[kind_index][layer_index] + summed[kind_index]
                )
            layer_parts[layer_index] = layer_parts[layer_index] + delta_vectors
        patch_part, token_part = embed_pull(back)
        grad_patch = grad_patch + lax.psum_scatter(
            patch_part.astype(jnp.bfloat16), "fsdp", scatter_dimension=1, tiled=True
        ).astype(jnp.float32)
        grad_token = grad_token + token_part
    grad_qkv, grad_out, grad_up, grad_down = tuple(
        (jnp.stack(grad_mats[kind_index]) for kind_index in range(4))
    )
    grad_layer = jnp.stack(layer_parts)
    sharded = (
        lax.psum(grad_patch.astype(jnp.bfloat16), "grp").astype(jnp.float32),
        lax.psum(grad_head.astype(jnp.bfloat16), "grp").astype(jnp.float32),
        lax.psum(grad_vocab.astype(jnp.bfloat16), "grp").astype(jnp.float32),
        lax.psum(grad_qkv.astype(jnp.bfloat16), "grp").astype(jnp.float32),
        lax.psum(grad_out.astype(jnp.bfloat16), "grp").astype(jnp.float32),
        lax.psum(grad_up.astype(jnp.bfloat16), "grp").astype(jnp.float32),
        lax.psum(grad_down.astype(jnp.bfloat16), "grp").astype(jnp.float32),
    )
    grad_token, grad_layer, loss_sum = lax.psum((grad_token, grad_layer, loss_sum), ("grp", "fsdp"))
    sharded_squares = jnp.zeros((), jnp.float32)
    for grad in sharded:
        sharded_squares = sharded_squares + jnp.sum(grad * grad)
    replicated_squares = jnp.sum(grad_token * grad_token) + jnp.sum(grad_layer * grad_layer)
    squares = lax.psum(sharded_squares + replicated_squares / lax.axis_size("fsdp"), "fsdp")
    clip_norm = jnp.sqrt(squares)
    clip_scale = jnp.minimum(1.0, clip_level / (clip_norm + 1e-06))
    updates = [
        adam_step(
            patch_weight,
            sharded[0] * clip_scale,
            first_patch,
            second_patch,
            weight_decay,
            matrix_rate,
        ),
        adam_step(
            head_weight, sharded[1] * clip_scale, first_head, second_head, weight_decay, matrix_rate
        ),
        adam_step(vocab_bias, sharded[2] * clip_scale, first_vocab, second_vocab, 0.0, vector_rate),
        adam_step(
            token_vectors, grad_token * clip_scale, first_token, second_token, 0.0, vector_rate
        ),
    ]
    matrices = [
        (qkv_weight, first_qkv, second_qkv),
        (out_weight, first_out, second_out),
        (up_weight, first_up, second_up),
        (down_weight, first_down, second_down),
    ]
    group_index = lax.axis_index("grp")
    for matrix_kind in range(4):
        weight_all, moment_all, square_all = matrices[matrix_kind]
        grad_all = sharded[3 + matrix_kind]
        results = []
        for layer_index in range(layers):
            slot = 4 * layer_index + matrix_kind
            current = (weight_all[layer_index], moment_all[layer_index], square_all[layer_index])

            def compute(
                current=current,
                grad=grad_all[layer_index] * clip_scale,
                basis=bases[slot],
                on_left=matrix_kind < 3,
            ):
                return rotated_step(current[0], grad, current[1], current[2], basis, on_left)

            result = lax.cond(owners[slot] == group_index, compute, lambda current=current: current)
            result = (
                spread_2(result[0].astype(jnp.bfloat16), "grp", owners[slot]).astype(jnp.float32),
                spread_2(result[1].astype(jnp.bfloat16), "grp", owners[slot]).astype(jnp.float32),
                spread_2(result[2].astype(jnp.bfloat16), "grp", owners[slot]).astype(jnp.float32),
            )
            results.append(result)
        updates.append(
            tuple((jnp.stack([result[member] for result in results]) for member in range(3)))
        )
    updates.append(
        adam_step(
            layer_vectors, grad_layer * clip_scale, first_layer, second_layer, 0.0, vector_rate
        )
    )
    return (
        loss_sum,
        clip_norm,
        *[entry[0] for entry in updates],
        *[entry[1] for entry in updates],
        *[entry[2] for entry in updates],
    )


def solution(mesh):
    placed = (
        P(("grp", "fsdp"), None, None),
        P(("grp", "fsdp"), None),
        P(("grp", "fsdp"), None),
        P(),
        P(),
        P(None, "fsdp"),
        P(None, "fsdp"),
        P("fsdp"),
        P(),
        P(None, None, "fsdp"),
        P(None, None, "fsdp"),
        P(None, None, "fsdp"),
        P(None, "fsdp", None),
        P(),
        P(None, "fsdp"),
        P(None, "fsdp"),
        P("fsdp"),
        P(),
        P(None, None, "fsdp"),
        P(None, None, "fsdp"),
        P(None, None, "fsdp"),
        P(None, "fsdp", None),
        P(),
        P(None, "fsdp"),
        P(None, "fsdp"),
        P("fsdp"),
        P(),
        P(None, None, "fsdp"),
        P(None, None, "fsdp"),
        P(None, None, "fsdp"),
        P(None, "fsdp", None),
        P(),
    )
    return jax.shard_map(
        body,
        mesh=mesh,
        in_specs=placed,
        out_specs=(
            P(),
            P(),
            P(None, "fsdp"),
            P(None, "fsdp"),
            P("fsdp"),
            P(),
            P(None, None, "fsdp"),
            P(None, None, "fsdp"),
            P(None, None, "fsdp"),
            P(None, "fsdp", None),
            P(),
            P(None, "fsdp"),
            P(None, "fsdp"),
            P("fsdp"),
            P(),
            P(None, None, "fsdp"),
            P(None, None, "fsdp"),
            P(None, None, "fsdp"),
            P(None, "fsdp", None),
            P(),
            P(None, "fsdp"),
            P(None, "fsdp"),
            P("fsdp"),
            P(),
            P(None, None, "fsdp"),
            P(None, None, "fsdp"),
            P(None, None, "fsdp"),
            P(None, "fsdp", None),
            P(),
        ),
        check_vma=False,
    )
```

profile of v0, /device:TPU:0, one launch (start us, length us, event | category | flops | bytes accessed | tf_op | source)
XLA Modules:
  0.0 3349.5 jit_solution(4192975915638828845)
XLA Ops:
  33.5 18.7 convolution_bitcast_fusion.1
  52.2 23.1 copy.677
  94.7 18.3 convolution_bitcast_fusion
  113.0 23.1 copy.690
  160.3 46.2 %all-gather.22.cloned.1.call-done = bf16[768,2304]{0,1:T(8,128)(2,1)} async-done(((bf16[768,288]{0,1:T(8,128)(2,1)}), bf16[768,2304]{0,1:T(8,128)(2,1)}) %all-gather.22.cloned.1.call-update) | async-done | bytes 3538960 | tf_op jit(solution)/shard_map/all_gather | solution.py:284
  224.9 47.9 %all-gather.30.cloned.1.call-done = bf16[768,2304]{0,1:T(8,128)(2,1)} async-done(((bf16[768,288]{0,1:T(8,128)(2,1)}), bf16[768,2304]{0,1:T(8,128)(2,1)}) %all-gather.30.cloned.1.call-update) | async-done | bytes 3538960 | tf_op jit(solution)/shard_map/all_gather | solution.py:284
  272.8 81.0 %all-gather.26.cloned.1.call-done = bf16[768,3072]{0,1:T(8,128)(2,1)} async-done(((bf16[768,384]{0,1:T(8,128)(2,1)}), bf16[768,3072]{0,1:T(8,128)(2,1)}) %all-gather.26.cloned.1.call-update) | async-done | bytes 4718608 | tf_op jit(solution)/shard_map/all_gather | solution.py:290
  353.8 16.0 multiply_convert_fusion.7
  369.9 64.8 %all-gather.28.cloned.1.call-done = bf16[3072,768]{1,0:T(8,128)(2,1)} async-done(((bf16[384,768]{1,0:T(8,128)(2,1)}), bf16[3072,768]{1,0:T(8,128)(2,1)}) %all-gather.28.cloned.1.call-update) | async-done | bytes 4718608 | tf_op jit(solution)/shard_map/all_gather | solution.py:293
  458.6 56.9 %all-gather.34.cloned.1.call-done = bf16[768,3072]{0,1:T(8,128)(2,1)} async-done(((bf16[768,384]{0,1:T(8,128)(2,1)}), bf16[768,3072]{0,1:T(8,128)(2,1)}) %all-gather.34.cloned.1.call-update) | async-done | bytes 4718608 | tf_op jit(solution)/shard_map/all_gather | solution.py:290
  515.5 15.7 multiply_convert_fusion.6
  531.2 65.1 %all-gather.36.cloned.1.call-done = bf16[3072,768]{1,0:T(8,128)(2,1)} async-done(((bf16[384,768]{1,0:T(8,128)(2,1)}), bf16[3072,768]{1,0:T(8,128)(2,1)}) %all-gather.36.cloned.1.call-update) | async-done | bytes 4718608 | tf_op jit(solution)/shard_map/all_gather | solution.py:293
  611.9 35.5 %all-reduce.98 = (s32[1200]{0:T(1024)S(1)}, s32[1200]{0:T(1024)}) all-reduce(s32[1200]{0:T(1024)S(1)} %dynamic-update-slice.2, s32[1200]{0:T(1024)S(1)} %dynamic-update-slice.6), channel_id=1, replica_groups=mesh['grp'=4,'fsdp'=8] {'fsdp'}, use_global_device_ids=true, to_apply=%add.88 | all-reduce | flops 2400 | bytes 19200
  664.6 69.0 %all-reduce.114.cloned.1.call-done = (f32[9600]{0:T(1024)}, f32[9600]{0:T(1024)}, f32[9600]{0:T(1024)}) async-done(((f32[9600]{0:T(1024)}, f32[9600]{0:T(1024)}, f32[9600]{0:T(1024)}), (f32[9600]{0:T(1024)}, f32[9600]{0:T(1024)}, f32[9600]{0:T(1024)})) %all-reduce.114.cloned.1.call-update) | async-done | bytes 115216
  747.9 78.6 %fusion = f32[152,768]{1,0:T(8,128)S(1)} fusion(f32[1200,768]{1,0:T(8,128)} %fusion.599), kind=kCustom, calls=%all-reduce-scatter | all-reduce-scatter fusion | flops 933889 | bytes 4153856
  926.7 14.3 multiply_convert_fusion.5
  962.4 14.4 multiply_convert_fusion.4
  983.0 48.4 %all-gather.40.cloned.1.call-done = bf16[8,150,768]{2,1,0:T(8,128)(2,1)} async-done(((bf16[1,150,768]{2,1,0:T(8,128)(2,1)}), bf16[8,150,768]{2,1,0:T(8,128)(2,1)}) %all-gather.40.cloned.1.call-update) | async-done | bytes 1843216 | tf_op jit(solution)/shard_map/all_gather | solution.py:307
  1048.8 65.8 %all-reduce.112.cloned.1.call-done = (f32[9600]{0:T(1024)}, f32[9600]{0:T(1024)}, f32[9600]{0:T(1024)}) async-done(((f32[9600]{0:T(1024)}, f32[9600]{0:T(1024)}, f32[9600]{0:T(1024)}), (f32[9600]{0:T(1024)}, f32[9600]{0:T(1024)}, f32[9600]{0:T(1024)})) %all-reduce.112.cloned.1.call-update) | async-done | bytes 115216
  1132.2 78.7 %fusion.1 = f32[152,768]{1,0:T(8,128)S(1)} fusion(f32[1200,768]{1,0:T(8,128)} %fusion.600), kind=kCustom, calls=%all-reduce-scatter.1 | all-reduce-scatter fusion | flops 933889 | bytes 4153856
  1453.8 12.9 reshape.1033
  1466.7 29.5 copy.767
  1496.2 17.4 fusion.382
  1537.6 29.9 copy.777
  1567.4 17.3 fusion.388
  1618.5 12.9 reshape.1034
  1631.4 29.6 copy.772
  1660.9 17.4 fusion.385
  1692.7 12.9 reshape.1036
  1705.6 29.5 copy.782
  1735.0 17.5 fusion.391
  1770.3 36.6 %reduce-scatter.63.cloned.1.call-done = bf16[384,768]{1,0:T(8,128)(2,1)} async-done(((bf16[3072,768]{1,0:T(8,128)(2,1)}), bf16[384,768]{1,0:T(8,128)(2,1)}) %reduce-scatter.63.cloned.1.call-update) | async-done | bytes 589840
  1808.3 81.2 %reduce-scatter.35.cloned.1.call-done = bf16[768,288]{0,1:T(8,128)(2,1)} async-done(((bf16[768,2304]{0,1:T(8,128)(2,1)}), bf16[768,288]{0,1:T(8,128)(2,1)}) %reduce-scatter.35.cloned.1.call-update) | async-done | bytes 442384 | tf_op jit(solution)/shard_map/reduce_scatter | solution.py:355
  1889.5 82.1 %reduce-scatter.37.cloned.1.call-done = bf16[768,288]{0,1:T(8,128)(2,1)} async-done(((bf16[768,2304]{0,1:T(8,128)(2,1)}), bf16[768,288]{0,1:T(8,128)(2,1)}) %reduce-scatter.37.cloned.1.call-update) | async-done | bytes 442384 | tf_op jit(solution)/shard_map/reduce_scatter | solution.py:355
  1972.8 81.0 %reduce-scatter.39.cloned.1.call-done = bf16[768,288]{0,1:T(8,128)(2,1)} async-done(((bf16[768,2304]{0,1:T(8,128)(2,1)}), bf16[768,288]{0,1:T(8,128)(2,1)}) %reduce-scatter.39.cloned.1.call-update) | async-done | bytes 442384 | tf_op jit(solution)/shard_map/reduce_scatter | solution.py:355
  2053.8 82.3 %reduce-scatter.41.cloned.1.call-done = bf16[768,288]{0,1:T(8,128)(2,1)} async-done(((bf16[768,2304]{0,1:T(8,128)(2,1)}), bf16[768,288]{0,1:T(8,128)(2,1)}) %reduce-scatter.41.cloned.1.call-update) | async-done | bytes 442384 | tf_op jit(solution)/shard_map/reduce_scatter | solution.py:355
  2138.4 96.3 %reduce-scatter.61.cloned.1.call-done = bf16[384,768]{1,0:T(8,128)(2,1)} async-done(((bf16[3072,768]{1,0:T(8,128)(2,1)}), bf16[384,768]{1,0:T(8,128)(2,1)}) %reduce-scatter.61.cloned.1.call-update) | async-done | bytes 589840
  2236.0 97.3 %reduce-scatter.65.cloned.1.call-done = bf16[384,768]{1,0:T(8,128)(2,1)} async-done(((bf16[3072,768]{1,0:T(8,128)(2,1)}), bf16[384,768]{1,0:T(8,128)(2,1)}) %reduce-scatter.65.cloned.1.call-update) | async-done | bytes 589840
  2334.7 97.5 %reduce-scatter.51.cloned.1.call-done = bf16[384,768]{1,0:T(8,128)(2,1)} async-done(((bf16[3072,768]{1,0:T(8,128)(2,1)}), bf16[384,768]{1,0:T(8,128)(2,1)}) %reduce-scatter.51.cloned.1.call-update) | async-done | bytes 589840 | tf_op jit(solution)/shard_map/reduce_scatter | solution.py:364
  2432.2 98.7 %reduce-scatter.53.cloned.1.call-done = bf16[384,768]{1,0:T(8,128)(2,1)} async-done(((bf16[3072,768]{1,0:T(8,128)(2,1)}), bf16[384,768]{1,0:T(8,128)(2,1)}) %reduce-scatter.53.cloned.1.call-update) | async-done | bytes 589840 | tf_op jit(solution)/shard_map/reduce_scatter | solution.py:364
  2532.2 97.3 %reduce-scatter.55.cloned.1.call-done = bf16[384,768]{1,0:T(8,128)(2,1)} async-done(((bf16[3072,768]{1,0:T(8,128)(2,1)}), bf16[384,768]{1,0:T(8,128)(2,1)}) %reduce-scatter.55.cloned.1.call-update) | async-done | bytes 589840 | tf_op jit(solution)/shard_map/reduce_scatter | solution.py:364
  2629.6 98.9 %reduce-scatter.57.cloned.1.call-done = bf16[384,768]{1,0:T(8,128)(2,1)} async-done(((bf16[3072,768]{1,0:T(8,128)(2,1)}), bf16[384,768]{1,0:T(8,128)(2,1)}) %reduce-scatter.57.cloned.1.call-update) | async-done | bytes 589840 | tf_op jit(solution)/shard_map/reduce_scatter | solution.py:364
  2755.8 39.9 %all-reduce.99 = (f32[]{:T(128)}, f32[5,768]{1,0:T(8,128)S(1)}) all-reduce(f32[]{:T(128)S(6)} %add.1363, f32[5,768]{1,0:T(8,128)S(1)} %add_add_fusion.20), channel_id=1, replica_groups=mesh['grp'=4,'fsdp'=8] {'grp','fsdp'}, use_global_device_ids=true, to_apply=%region_42.0 | all-reduce | flops 3841 | bytes 30728 | tf_op jit(solution)/shard_map/psum | solution.py:391
  2796.3 59.7 %all-reduce.110.cloned.1.call-done = f32[2,19536]{1,0:T(2,128)} async-done(((f32[2,19536]{1,0:T(2,128)}), f32[2,19536]{1,0:T(2,128)}) %all-reduce.110.cloned.1.call-update) | async-done | bytes 156304 | tf_op jit(solution)/shard_map/psum | solution.py:391
  2858.9 107.3 %all-reduce.118.cloned.1.call-done = (bf16[768,96]{0,1:T(8,128)(2,1)}, bf16[768,1024]{1,0:T(8,128)(2,1)}, bf16[2,768,288]{1,2,0:T(8,128)(2,1)}, bf16[2,768,96]{1...) async-done(((bf16[768,96]{0,1:T(8,128)(2,1)}, bf16[768,1024]{1,0:T(8,128)(2,1)}, bf16[2,768,288]{1,2,0:T(8,128)(2,1)}, ...) | async-done | bytes 5259280 | tf_op jit(solution)/shard_map/psum | solution.py:383
  2983.3 21.9 psum.255
  3065.9 14.7 conditional.9
  3098.0 225.7 %all-reduce.116.cloned.1.call-done = (bf16[1,768,288]{1,2,0:T(8,128)(2,1)}, bf16[1,768,288]{1,2,0:T(8,128)(2,1)}, bf16[1,768,96]{1,2,0:T(8,128)(2,1)}, bf16[1,76...) async-done(((bf16[1,768,288]{1,2,0:T(8,128)(2,1)}, ...) | async-done | bytes 10616848 | tf_op jit(solution)/shard_map/psum | solution.py:42
  (1569 shorter events, 797.2 us)
Async XLA Ops:
  7.2 147.1 %all-gather.20.cloned.1.call-start = ((), (), s32[]{:S(2)}) async-start(), calls=%async_computation.18 | async-start | bytes 1327104 | tf_op jit(solution)/shard_map/all_gather | solution.py:271
  9.1 151.2 %all-gather.24.cloned.1.call-start = ((), (), s32[]{:S(2)}) async-start(), calls=%async_computation.20 | async-start | bytes 1327104 | tf_op jit(solution)/shard_map/all_gather | solution.py:287
  10.9 149.3 %all-gather.32.cloned.1.call-start = ((), (), s32[]{:S(2)}) async-start(), calls=%async_computation.24 | async-start | bytes 1327104 | tf_op jit(solution)/shard_map/all_gather | solution.py:287
  11.7 194.8 %all-gather.22.cloned.1.call-start = ((), (), s32[]{:S(2)}) async-start(), calls=%async_computation.19 | async-start | bytes 3981312 | tf_op jit(solution)/shard_map/all_gather | solution.py:284
  14.2 258.6 %all-gather.30.cloned.1.call-start = ((), (), s32[]{:S(2)}) async-start(), calls=%async_computation.23 | async-start | bytes 3981312 | tf_op jit(solution)/shard_map/all_gather | solution.py:284
  14.8 339.0 %all-gather.26.cloned.1.call-start = ((), (), s32[]{:S(2)}) async-start(), calls=%async_computation.21 | async-start | bytes 5308416 | tf_op jit(solution)/shard_map/all_gather | solution.py:290
  19.2 415.4 %all-gather.28.cloned.1.call-start = ((), (), s32[]{:S(2)}) async-start(), calls=%async_computation.22 | async-start | bytes 5308416 | tf_op jit(solution)/shard_map/all_gather | solution.py:293
  20.4 495.0 %all-gather.34.cloned.1.call-start = ((), (), s32[]{:S(2)}) async-start(), calls=%async_computation.25 | async-start | bytes 5308416 | tf_op jit(solution)/shard_map/all_gather | solution.py:290
  25.5 570.8 %all-gather.36.cloned.1.call-start = ((), (), s32[]{:S(2)}) async-start(), calls=%async_computation.26 | async-start | bytes 5308416 | tf_op jit(solution)/shard_map/all_gather | solution.py:293
  26.2 624.1 %all-gather.38.cloned.1.call-start = ((), (), s32[]{:S(2)}) async-start(), calls=%async_computation.42 | async-start | bytes 2101248 | tf_op jit(solution)/shard_map/all_gather | solution.py:307
  27.6 194.8 %copy-start.239 = (f32[768]{0:T(1024)}, f32[768]{0:T(1024)S(1)}, u32[]{:S(2)}) copy-start(f32[768]{0:T(1024)S(1)} %get-tuple-element.1091) | copy-start | bytes 9220
  27.6 197.0 %copy-start.212 = (f32[768]{0:T(1024)}, f32[768]{0:T(1024)S(1)}, u32[]{:S(2)}) copy-start(f32[768]{0:T(1024)S(1)} %get-tuple-element.1084) | copy-start | bytes 9220
  27.6 197.0 %copy-start.286 = (f32[768]{0:T(1024)}, f32[768]{0:T(1024)S(1)}, u32[]{:S(2)}) copy-start(f32[768]{0:T(1024)S(1)} %get-tuple-element.1083) | copy-start | bytes 9220
  27.6 407.1 %copy-start.271 = (f32[768]{0:T(1024)}, f32[768]{0:T(1024)S(1)}, u32[]{:S(2)}) copy-start(f32[768]{0:T(1024)S(1)} %get-tuple-element.1085) | copy-start | bytes 9220
  27.6 413.7 %copy-start.284 = (f32[768]{0:T(1024)}, f32[768]{0:T(1024)S(1)}, u32[]{:S(2)}) copy-start(f32[768]{0:T(1024)S(1)} %get-tuple-element.1079) | copy-start | bytes 9220
  27.6 428.4 %copy-start.280 = (f32[768]{0:T(1024)}, f32[768]{0:T(1024)S(1)}, u32[]{:S(2)}) copy-start(f32[768]{0:T(1024)S(1)} %get-tuple-element.1076) | copy-start | bytes 9220
  27.6 430.7 %copy-start.278 = (f32[768]{0:T(1024)}, f32[768]{0:T(1024)S(1)}, u32[]{:S(2)}) copy-start(f32[768]{0:T(1024)S(1)} %get-tuple-element.1074) | copy-start | bytes 9220
  154.3 287.3 %copy-start.388 = (f32[2304]{0:T(1024)}, f32[2304]{0:T(1024)S(1)}, u32[]{:S(2)}) copy-start(f32[2304]{0:T(1024)S(1)} %get-tuple-element.1313) | copy-start | bytes 27652
  224.3 210.4 %copy-start.10 = (f32[2,197,768]{2,1,0:T(8,128)}, f32[2,197,768]{2,1,0:T(8,128)S(1)}, u32[]{:S(2)}) copy-start(f32[2,197,768]{2,1,0:T(8,128)S(1)} %get-tuple-element.1238) | copy-start | bytes 3631108
  224.3 145.5 %copy-start.256 = (f32[2,197]{1,0:T(2,128)}, f32[2,197]{1,0:T(2,128)S(1)}, u32[]{:S(2)}) copy-start(f32[2,197]{1,0:T(2,128)S(1)} %broadcast_multiply_fusion.8) | copy-start | bytes 4732
  224.6 145.3 %copy-start.321 = (f32[2,197]{1,0:T(2,128)}, f32[2,197]{1,0:T(2,128)S(1)}, u32[]{:S(2)}) copy-start(f32[2,197]{1,0:T(2,128)S(1)} %multiply_reduce_fusion.45) | copy-start | bytes 4732
  224.6 145.3 %copy-start.293 = (f32[2,197]{1,0:T(2,128)}, f32[2,197]{1,0:T(2,128)S(1)}, u32[]{:S(2)}) copy-start(f32[2,197]{1,0:T(2,128)S(1)} %fusion.527) | copy-start | bytes 4732
  605.2 128.4 %all-reduce.114.cloned.1.call-start = ((), (), s32[]{:S(2)}) async-start(), calls=%async_computation.49 | async-start | bytes 245760
  664.5 366.9 %all-gather.40.cloned.1.call-start = ((), (), s32[]{:S(2)}) async-start(), calls=%async_computation.43 | async-start | bytes 2101248 | tf_op jit(solution)/shard_map/all_gather | solution.py:307
  826.6 4.3 collective-permute-start
  983.0 131.6 %all-reduce.112.cloned.1.call-start = ((), (), s32[]{:S(2)}) async-start(), calls=%async_computation.48 | async-start | bytes 245760
  1045.6 718.7 %reduce-scatter.43.cloned.1.call-start = ((), (), s32[]{:S(2)}) async-start(), calls=%async_computation.33 | async-start | bytes 1327104 | tf_op jit(solution)/shard_map/reduce_scatter | solution.py:358
  1210.9 4.3 collective-permute-start.1
  1214.1 550.2 %reduce-scatter.45.cloned.1.call-start = ((), (), s32[]{:S(2)}) async-start(), calls=%async_computation.34 | async-start | bytes 1327104 | tf_op jit(solution)/shard_map/reduce_scatter | solution.py:358
  1278.9 486.5 %reduce-scatter.47.cloned.1.call-start = ((), (), s32[]{:S(2)}) async-start(), calls=%async_computation.35 | async-start | bytes 1327104 | tf_op jit(solution)/shard_map/reduce_scatter | solution.py:358
  1281.5 483.9 %reduce-scatter.49.cloned.1.call-start = ((), (), s32[]{:S(2)}) async-start(), calls=%async_computation.36 | async-start | bytes 1327104 | tf_op jit(solution)/shard_map/reduce_scatter | solution.py:358
  1299.0 468.2 %reduce-scatter.33.cloned.1.call-start = ((), (), s32[]{:S(2)}) async-start(), calls=%async_computation.28 | async-start | bytes 1327104 | tf_op jit(solution)/shard_map/reduce_scatter | solution.py:374
  1313.3 453.9 %reduce-scatter.31.cloned.1.call-start = ((), (), s32[]{:S(2)}) async-start(), calls=%async_computation.27 | async-start | bytes 1327104 | tf_op jit(solution)/shard_map/reduce_scatter | solution.py:374
  1318.3 450.6 %reduce-scatter.59.cloned.1.call-start = ((), (), s32[]{:S(2)}) async-start(), calls=%async_computation.44 | async-start | bytes 5308416
  1329.4 477.5 %reduce-scatter.63.cloned.1.call-start = ((), (), s32[]{:S(2)}) async-start(), calls=%async_computation.46 | async-start | bytes 5308416
  1342.2 547.2 %reduce-scatter.35.cloned.1.call-start = ((), (), s32[]{:S(2)}) async-start(), calls=%async_computation.29 | async-start | bytes 3981312 | tf_op jit(solution)/shard_map/reduce_scatter | solution.py:355
  1348.0 623.6 %reduce-scatter.37.cloned.1.call-start = ((), (), s32[]{:S(2)}) async-start(), calls=%async_computation.30 | async-start | bytes 3981312 | tf_op jit(solution)/shard_map/reduce_scatter | solution.py:355
  1353.6 700.2 %reduce-scatter.39.cloned.1.call-start = ((), (), s32[]{:S(2)}) async-start(), calls=%async_computation.31 | async-start | bytes 3981312 | tf_op jit(solution)/shard_map/reduce_scatter | solution.py:355
  1359.2 776.9 %reduce-scatter.41.cloned.1.call-start = ((), (), s32[]{:S(2)}) async-start(), calls=%async_computation.32 | async-start | bytes 3981312 | tf_op jit(solution)/shard_map/reduce_scatter | solution.py:355
  1365.8 868.9 %reduce-scatter.61.cloned.1.call-start = ((), (), s32[]{:S(2)}) async-start(), calls=%async_computation.45 | async-start | bytes 5308416
  1379.5 953.8 %reduce-scatter.65.cloned.1.call-start = ((), (), s32[]{:S(2)}) async-start(), calls=%async_computation.47 | async-start | bytes 5308416
  1393.2 1039.0 %reduce-scatter.51.cloned.1.call-start = ((), (), s32[]{:S(2)}) async-start(), calls=%async_computation.37 | async-start | bytes 5308416 | tf_op jit(solution)/shard_map/reduce_scatter | solution.py:364
  1400.8 1130.1 %reduce-scatter.53.cloned.1.call-start = ((), (), s32[]{:S(2)}) async-start(), calls=%async_computation.38 | async-start | bytes 5308416 | tf_op jit(solution)/shard_map/reduce_scatter | solution.py:364
  1408.4 1221.1 %reduce-scatter.55.cloned.1.call-start = ((), (), s32[]{:S(2)}) async-start(), calls=%async_computation.39 | async-start | bytes 5308416 | tf_op jit(solution)/shard_map/reduce_scatter | solution.py:364
  1416.0 1312.4 %reduce-scatter.57.cloned.1.call-start = ((), (), s32[]{:S(2)}) async-start(), calls=%async_computation.40 | async-start | bytes 5308416 | tf_op jit(solution)/shard_map/reduce_scatter | solution.py:364
  1599.8 1256.1 %all-reduce.110.cloned.1.call-start = ((), (), s32[]{:S(2)}) async-start(), calls=%async_computation.41 | async-start | bytes 313344 | tf_op jit(solution)/shard_map/psum | solution.py:391
  1763.8 1202.4 %all-reduce.118.cloned.1.call-start = ((), (), s32[]{:S(2)}) async-start(), calls=%async_computation.51 | async-start | bytes 10518528 | tf_op jit(solution)/shard_map/psum | solution.py:383
  2732.4 591.3 %all-reduce.116.cloned.1.call-start = ((), (), s32[]{:S(2)}) async-start(), calls=%async_computation.50 | async-start | bytes 21233664 | tf_op jit(solution)/shard_map/psum | solution.py:42
  (440 other events, 4039.4 us)
Sparse Core Ops, SparseCore 0:
  10.8 43.7 all-gather.19
  57.3 39.8 all-gather.23
  100.0 39.8 all-gather.31
  142.5 63.9 all-gather.21
  209.1 63.6 all-gather.29
  275.4 78.3 all-gather.25
  356.6 78.0 all-gather.27
  437.4 78.0 all-gather.33
  518.2 78.0 all-gather.35
  605.3 44.9 all-gather.37
  664.6 68.8 all-reduce.113
  983.1 48.2 all-gather.39
  1045.7 68.8 all-reduce.111
  1214.2 63.4 reduce-scatter.42
  1281.0 63.6 reduce-scatter.44
  1347.9 62.9 reduce-scatter.46
  1414.1 63.1 reduce-scatter.48
  1480.5 63.1 reduce-scatter.32
  1547.1 63.1 reduce-scatter.30
  1613.7 94.2 reduce-scatter.58
  1711.7 95.1 reduce-scatter.62
  1810.5 78.8 reduce-scatter.34
  1893.1 78.4 reduce-scatter.36
  1975.1 78.6 reduce-scatter.38
  2057.4 78.6 reduce-scatter.40
  2139.6 94.9 reduce-scatter.60
  2238.1 95.1 reduce-scatter.64
  2337.0 95.1 reduce-scatter.50
  2435.8 94.9 reduce-scatter.52
  2534.3 95.1 reduce-scatter.54
  2633.2 95.1 reduce-scatter.56
  2734.6 121.3 all-reduce.109
  2860.3 105.8 all-reduce.117
  3088.2 235.4 all-reduce.115
where the time goes:
time: 3370 us; the launch traced here: 3350 us
  waiting for transfers between devices  1890 us (56%)
  local copies, waits for them, and re-layouts  469 us (14%)
  matrix products  454 us (13%)
  blocking collectives  261 us (8%)
  other arithmetic  218 us (6%)
  between operations  41.7 us (1%)
    reduce_scatter x4, waiting for transfers between devices, body(): lax.psum_scatter(delta_down.astype(jnp.bfloat16), 'fsdp', scatter_dimensi...  392 us
    unnamed x42, waiting for transfers between devices  369 us
    reduce_scatter x4, waiting for transfers between devices, body(): lax.psum_scatter(delta_qkv.astype(jnp.bfloat16), 'fsdp', scatter_dimensio...  327 us
    dot_general x60, matrix products, product(): jnp.dot(left_side, right_side, precision=highest, preferred_element_type=...  280 us
    psum x1, waiting for transfers between devices, spread_2(): return lax.psum(block, axis)  226 us
    reshape x10, local copies, waits for them, and re-layouts, position_bias(): jnp.einsum('hrxw,yvr->hyxvw', along, pick, precision=highest)  195 us
    unnamed x3, blocking collectives  193 us
    all_gather x2, waiting for transfers between devices, body(): lax.all_gather(up_weight[layer_index].astype(jnp.bfloat16), 'fsdp', axis=...  138 us
  transfers between devices with their start and end apart: 36, of which 26 were waited for; matrix products, arithmetic and copies ran while one was open for 23% of the time, Pallas kernels for 0%

commit v1 on v0

v1 whole, which is shorter than its diff:
```python
import functools

import jax
import jax.numpy as jnp
from jax import lax
from jax.experimental import pallas as pl
from jax.experimental.pallas import tpu as pltpu
from jax.sharding import PartitionSpec as P

D = 768
H = 12
HD = 64
FF = 3072
SIDE = 14
SPAN = 2 * SIDE - 1
FAR = SPAN * SPAN
NMASK = 75
STEP = 10
NPATCH = 196
NREL = 732
TOK = 208
STRIP = 384
RELPAD = 736

beta_one = 0.9
beta_two = 0.999
adam_eps = 1e-08
matrix_rate = 0.06
vector_rate = 0.5
weight_decay = 0.05
clip_level = 1.0
norm_eps = 1e-06

BF = jnp.bfloat16
F32 = jnp.float32
NN = (((1,), (0,)), ((), ()))
NT = (((1,), (1,)), ((), ()))
TN = (((0,), (0,)), ((), ()))


def dot(a, b, dims=NN):
    return lax.dot_general(a, b, dims, preferred_element_type=F32)


def three_parts(value):
    high = value.astype(BF)
    rest = value - high.astype(F32)
    middle = rest.astype(BF)
    return high, middle, (rest - middle.astype(F32)).astype(BF)


def one_hot_strip(xa):
    slot = lax.broadcasted_iota(jnp.int32, (RELPAD, STRIP), 0)
    lane = lax.broadcasted_iota(jnp.int32, (1, STRIP), 1)
    wanted = (SPAN - 1 - lane // SIDE) * SPAN + xa - lane % SIDE + SIDE - 1
    wanted = jnp.where(lane < SPAN * SIDE, wanted, -1)
    return (slot == wanted).astype(BF)


def expand_kernel(table_ref, bias_ref, strip_ref):
    table = table_ref[...]
    parts = jnp.concatenate(three_parts(table), axis=0)
    rows = table.shape[0]
    for xa in range(SIDE):
        got = dot(parts, one_hot_strip(xa))
        strip_ref[:, xa, :] = got[:rows] + got[rows : 2 * rows] + got[2 * rows :]
    row = lax.broadcasted_iota(jnp.int32, (TOK, TOK), 0)
    col = lax.broadcasted_iota(jnp.int32, (TOK, TOK), 1)
    for h in range(H):
        strip = strip_ref[h]
        for ya in range(SIDE):
            start = (SIDE - 1 - ya) * SIDE
            turned = pltpu.roll(strip, (STRIP - start) % STRIP, 1)
            bias_ref[h, ya * SIDE : (ya + 1) * SIDE, :] = turned[:SIDE, :TOK]
        bias_ref[h, NPATCH:TOK, :] = jnp.zeros((TOK - NPATCH, TOK), F32)
        top = table[h : h + 1, FAR : FAR + 1]
        left = table[h : h + 1, FAR + 1 : FAR + 2]
        corner = table[h : h + 1, FAR + 2 : FAR + 3]
        value = bias_ref[h]
        value = jnp.where(row == NPATCH, top, value)
        value = jnp.where(col == NPATCH, jnp.where(row == NPATCH, corner, left), value)
        bias_ref[h] = jnp.where(col > NPATCH, -1e30, value)


def expand_bias(table):
    padded = jnp.pad(table, ((0, 16 - H), (0, RELPAD - NREL)))
    return pl.pallas_call(
        expand_kernel,
        out_shape=jax.ShapeDtypeStruct((H, TOK, TOK), F32),
        in_specs=[pl.BlockSpec(memory_space=pltpu.VMEM)],
        out_specs=pl.BlockSpec(memory_space=pltpu.VMEM),
        scratch_shapes=[pltpu.VMEM((16, 16, STRIP), F32)],
        compiler_params=pltpu.CompilerParams(vmem_limit_bytes=48 << 20),
    )(padded)


def reduce_kernel(grad_ref, table_ref, strip_ref):
    lane = lax.broadcasted_iota(jnp.int32, (SIDE, STRIP), 1)
    row = lax.broadcasted_iota(jnp.int32, (TOK, TOK), 0)
    col = lax.broadcasted_iota(jnp.int32, (TOK, TOK), 1)
    slots = lax.broadcasted_iota(jnp.int32, (1, RELPAD), 1)
    strip_ref[...] = jnp.zeros_like(strip_ref)
    for h in range(H):
        total = jnp.zeros((SIDE, STRIP), F32)
        for ya in range(SIDE):
            start = (SIDE - 1 - ya) * SIDE
            window = grad_ref[h, ya * SIDE : (ya + 1) * SIDE, :]
            window = jnp.concatenate(
                [window, jnp.zeros((SIDE, STRIP - TOK), F32)], axis=1
            )
            window = jnp.where(lane < NPATCH, window, 0.0)
            total = total + pltpu.roll(window, start, 1)
        strip_ref[h, :SIDE, :] = total
    acc = jnp.zeros((16, RELPAD), F32)
    for xa in range(SIDE):
        high, middle, unused = three_parts(strip_ref[:, xa, :])
        got = dot(jnp.concatenate([high, middle], axis=0), one_hot_strip(xa), NT)
        acc = acc + got[:16] + got[16:]
    for h in range(H):
        value = grad_ref[h]
        top = jnp.where((row == NPATCH) & (col < NPATCH), value, 0.0)
        left = jnp.where((col == NPATCH) & (row < NPATCH), value, 0.0)
        corner = jnp.where((col == NPATCH) & (row == NPATCH), value, 0.0)
        extra = jnp.where(slots == FAR, jnp.sum(top, keepdims=True), 0.0)
        extra = extra + jnp.where(slots == FAR + 1, jnp.sum(left, keepdims=True), 0.0)
        extra = extra + jnp.where(slots == FAR + 2, jnp.sum(corner, keepdims=True), 0.0)
        table_ref[h : h + 1, :] = acc[h : h + 1] + extra


def reduce_bias(grad):
    table = pl.pallas_call(
        reduce_kernel,
        out_shape=jax.ShapeDtypeStruct((16, RELPAD), F32),
        in_specs=[pl.BlockSpec(memory_space=pltpu.VMEM)],
        out_specs=pl.BlockSpec(memory_space=pltpu.VMEM),
        scratch_shapes=[pltpu.VMEM((16, 16, STRIP), F32)],
        compiler_params=pltpu.CompilerParams(vmem_limit_bytes=48 << 20),
    )(grad)
    return table[:H, :NREL]


def attend_kernel(qkv_ref, bias_ref, out_ref, prob_ref):
    lane = lax.broadcasted_iota(jnp.int32, (1, 2 * HD), 1)
    for pair in range(H // 2):
        lo = pair * 2 * HD
        query = qkv_ref[:, lo : lo + 2 * HD]
        key = qkv_ref[:, D + lo : D + lo + 2 * HD]
        value = qkv_ref[:, 2 * D + lo : 2 * D + lo + 2 * HD]
        outs = []
        for side in range(2):
            mine = (lane // HD) == side
            scores = dot(jnp.where(mine, query, jnp.zeros_like(query)), key, NT)
            scores = scores * HD**-0.5 + bias_ref[2 * pair + side]
            scores = jnp.exp(scores - jnp.max(scores, axis=1, keepdims=True))
            total = jnp.sum(scores, axis=1, keepdims=True)
            prob = (scores * (1.0 / total)).astype(BF)
            prob_ref[0, 2 * pair + side] = prob
            outs.append(dot(prob, value))
        out_ref[:, lo : lo + 2 * HD] = jnp.where(lane < HD, outs[0], outs[1]).astype(BF)


def attend(qkv, bias):
    count = qkv.shape[0] // TOK
    return pl.pallas_call(
        attend_kernel,
        grid=(count,),
        out_shape=(
            jax.ShapeDtypeStruct((count * TOK, D), BF),
            jax.ShapeDtypeStruct((count, H, TOK, TOK), BF),
        ),
        in_specs=[
            pl.BlockSpec((TOK, 3 * D), lambda i: (i, 0)),
            pl.BlockSpec((H, TOK, TOK), lambda i: (0, 0, 0)),
        ],
        out_specs=(
            pl.BlockSpec((TOK, D), lambda i: (i, 0)),
            pl.BlockSpec((1, H, TOK, TOK), lambda i: (i, 0, 0, 0)),
        ),
        compiler_params=pltpu.CompilerParams(vmem_limit_bytes=48 << 20),
    )(qkv, bias)


def attend_back_kernel(qkv_ref, prob_ref, grad_ref, dqkv_ref, dbias_ref):
    lane = lax.broadcasted_iota(jnp.int32, (1, 2 * HD), 1)

    @pl.when(pl.program_id(0) == 0)
    def clear():
        dbias_ref[...] = jnp.zeros_like(dbias_ref)

    for pair in range(H // 2):
        lo = pair * 2 * HD
        query = qkv_ref[:, lo : lo + 2 * HD]
        key = qkv_ref[:, D + lo : D + lo + 2 * HD]
        value = qkv_ref[:, 2 * D + lo : 2 * D + lo + 2 * HD]
        grad = grad_ref[:, lo : lo + 2 * HD]
        queries, keys, values = [], [], []
        for side in range(2):
            mine = (lane // HD) == side
            prob = prob_ref[0, 2 * pair + side]
            dprob = dot(jnp.where(mine, grad, jnp.zeros_like(grad)), value, NT)
            wide = prob.astype(F32)
            both = wide * dprob
            dscore = both - wide * jnp.sum(both, axis=1, keepdims=True)
            dbias_ref[2 * pair + side] += dscore
            draw = (dscore * HD**-0.5).astype(BF)
            queries.append(dot(draw, key))
            keys.append(dot(draw, query, TN))
            values.append(dot(prob, grad, TN))
        for place, pieces in enumerate((queries, keys, values)):
            at = place * D + lo
            dqkv_ref[:, at : at + 2 * HD] = jnp.where(lane < HD, pieces[0], pieces[1]).astype(BF)


def attend_back(qkv, prob, grad):
    count = qkv.shape[0] // TOK
    return pl.pallas_call(
        attend_back_kernel,
        grid=(count,),
        out_shape=(
            jax.ShapeDtypeStruct((count * TOK, 3 * D), BF),
            jax.ShapeDtypeStruct((H, TOK, TOK), F32),
        ),
        in_specs=[
            pl.BlockSpec((TOK, 3 * D), lambda i: (i, 0)),
            pl.BlockSpec((1, H, TOK, TOK), lambda i: (i, 0, 0, 0)),
            pl.BlockSpec((TOK, D), lambda i: (i, 0)),
        ],
        out_specs=(
            pl.BlockSpec((TOK, 3 * D), lambda i: (i, 0)),
            pl.BlockSpec((H, TOK, TOK), lambda i: (0, 0, 0)),
        ),
        compiler_params=pltpu.CompilerParams(vmem_limit_bytes=48 << 20),
    )(qkv, prob, grad)


def normal_parts(values):
    centered = values - jnp.mean(values, axis=-1, keepdims=True)
    spread = jnp.mean(centered * centered, axis=-1, keepdims=True)
    scale = lax.rsqrt(spread + norm_eps)
    return centered * scale, scale


def layer_norm(values, gain_row, bias_row):
    return (normal_parts(values)[0] * gain_row + bias_row).astype(BF)


def layer_norm_back(values, gain_row, grad):
    normal, scale = normal_parts(values)
    inner = grad * gain_row
    mean_one = jnp.mean(inner, axis=-1, keepdims=True)
    mean_two = jnp.mean(inner * normal, axis=-1, keepdims=True)
    back = (inner - mean_one - normal * mean_two) * scale
    return back, jnp.sum(grad * normal, axis=0), jnp.sum(grad, axis=0)


def unpack(vectors):
    pieces = [vectors[slot * D : (slot + 1) * D] for slot in range(10)]
    fc_bias = vectors[10 * D : 10 * D + FF]
    bias_table = vectors[10 * D + FF :].reshape(H, NREL)
    return (pieces, fc_bias, bias_table)


def layer_forward(states, full, vectors, bias):
    qkv_full, out_full, up_full, down_full = full
    pieces, fc_bias, unused = unpack(vectors)
    (gain_one, bias_one, query_bias, value_bias, out_bias) = pieces[:5]
    (scale_one, gain_two, bias_two, down_bias, scale_two) = pieces[5:]
    qkv_bias = jnp.concatenate([query_bias, jnp.zeros_like(query_bias), value_bias])
    normed = layer_norm(states, gain_one, bias_one)
    qkv = (dot(normed, qkv_full, NT) + qkv_bias).astype(BF)
    attended, prob = attend(qkv, bias)
    first = dot(attended, out_full, NT) + out_bias
    mid = states + scale_one * first
    normed_two = layer_norm(mid, gain_two, bias_two)
    raised = dot(normed_two, up_full, NT) + fc_bias
    below = 0.5 + 0.5 * lax.erf(raised * 0.5**0.5)
    hidden = (raised * below).astype(BF)
    slope = (below + raised * jnp.exp(-0.5 * raised * raised) * 0.3989422804014327).astype(BF)
    second = dot(hidden, down_full) + down_bias
    kept = (states, normed, qkv, prob, attended, first.astype(BF), mid, normed_two)
    return mid + scale_two * second, kept + (hidden, slope, second.astype(BF))


def layer_back(grad, kept, full, vectors):
    states, normed, qkv, prob, attended, first, mid, normed_two, hidden, slope, second = kept
    qkv_full, out_full, up_full, down_full = full
    pieces, unused, unused_table = unpack(vectors)
    gain_one, scale_one, gain_two, scale_two = (pieces[0], pieces[5], pieces[6], pieces[9])
    dsecond = (grad * scale_two).astype(BF)
    dscale_two = jnp.sum(grad * second.astype(F32), axis=0)
    ddown_bias = jnp.sum(dsecond.astype(F32), axis=0)
    ddown = dot(hidden, dsecond, TN).astype(BF)
    draised = (dot(dsecond, down_full, NT) * slope.astype(F32)).astype(BF)
    dfc_bias = jnp.sum(draised.astype(F32), axis=0)
    dup = dot(draised, normed_two, TN).astype(BF)
    back, dgain_two, dbias_two = layer_norm_back(mid, gain_two, dot(draised, up_full))
    dmid = grad + back
    dfirst = (dmid * scale_one).astype(BF)
    dscale_one = jnp.sum(dmid * first.astype(F32), axis=0)
    dout_bias = jnp.sum(dfirst.astype(F32), axis=0)
    dout = dot(dfirst, attended, TN).astype(BF)
    dattended = dot(dfirst, out_full).astype(BF)
    dqkv, dbias = attend_back(qkv, prob, dattended)
    dtable = reduce_bias(dbias)
    dqkv_bias = jnp.sum(dqkv.astype(F32), axis=0)
    dqkv_weight = dot(dqkv, normed, TN).astype(BF)
    back, dgain_one, dbias_one = layer_norm_back(states, gain_one, dot(dqkv, qkv_full))
    pieces = [
        dgain_one,
        dbias_one,
        dqkv_bias[:D],
        dqkv_bias[2 * D :],
        dout_bias,
        dscale_one,
        dgain_two,
        dbias_two,
        ddown_bias,
        dscale_two,
        dfc_bias,
        dtable.reshape(-1),
    ]
    return dmid + back, (dqkv_weight, dout, dup, ddown), jnp.concatenate(pieces)


def adam_parts(grad, first_moment, second_moment):
    first_moment = beta_one * first_moment + (1 - beta_one) * grad
    second_moment = beta_two * second_moment + (1 - beta_two) * grad * grad
    update = (
        first_moment
        / (1 - beta_one**STEP)
        / (jnp.sqrt(second_moment / (1 - beta_two**STEP)) + adam_eps)
    )
    return update, first_moment, second_moment


def adam_step(weight, grad, first_moment, second_moment, decay, rate):
    update, first_moment, second_moment = adam_parts(grad, first_moment, second_moment)
    return (weight - rate * (update + decay * weight), first_moment, second_moment)


def product(left_side, right_side, dims=NN):
    return lax.dot_general(
        left_side, right_side, dims, precision=lax.Precision.HIGH, preferred_element_type=F32
    )


def gather_weights(shards):
    return [lax.all_gather(shard, "fsdp", axis=0, tiled=True) for shard in shards]


def gather_rows(rows):
    return lax.all_gather(rows, "fsdp", axis=0, tiled=True)


def gather_stats(stats):
    return lax.all_gather(stats, "fsdp")


def scatter_rows(grads):
    return lax.psum_scatter(grads, "fsdp", scatter_dimension=0, tiled=True).astype(F32)


def reduce_weights(grads):
    scattered = [
        lax.psum_scatter(grad, "fsdp", scatter_dimension=0, tiled=True) for grad in grads
    ]
    return [lax.psum(part, "grp").astype(F32) for part in scattered]


def body(
    patches,
    positions,
    codes,
    owners,
    bases,
    patch_weight,
    head_weight,
    vocab_bias,
    token_vectors,
    qkv_weight,
    out_weight,
    up_weight,
    down_weight,
    layer_vectors,
    first_patch,
    first_head,
    first_vocab,
    first_token,
    first_qkv,
    first_out,
    first_up,
    first_down,
    first_layer,
    second_patch,
    second_head,
    second_vocab,
    second_token,
    second_qkv,
    second_out,
    second_up,
    second_down,
    second_layer,
):
    layers = qkv_weight.shape[0]
    count = patches.shape[0]
    tokens = count * TOK
    picked = count * NMASK
    row_count = -(-picked // 16) * 16
    vocab_local = head_weight.shape[1]
    place = lax.axis_index("fsdp")
    vocab_ids = place * vocab_local + jnp.arange(vocab_local, dtype=jnp.int32)

    shards = [patch_weight.T.astype(BF)]
    for index in range(layers):
        shards += [
            qkv_weight[index].T.astype(BF),
            out_weight[index].T.astype(BF),
            up_weight[index].T.astype(BF),
            down_weight[index].astype(BF),
        ]
    gathered = gather_weights(shards)
    patch_full = gathered[0]
    full = [gathered[1 + 4 * index : 5 + 4 * index] for index in range(layers)]
    biases = [expand_bias(unpack(layer_vectors[index])[2]) for index in range(layers)]

    flat_patches = jnp.pad(patches, ((0, 0), (0, TOK - NPATCH), (0, 0))).reshape(tokens, D)
    slots = jnp.arange(TOK, dtype=jnp.int32)
    hit = (positions[:, :, None] - 1 == slots[None, None, :]).astype(F32)
    masked = jnp.sum(hit, axis=1).reshape(tokens, 1)
    slot_of = jnp.tile(slots, count)[:, None]
    is_patch = (slot_of < NPATCH).astype(F32)
    is_class = (slot_of == NPATCH).astype(F32)
    shown = is_patch * (1.0 - masked)
    states = (dot(flat_patches, patch_full, NT) + token_vectors[0]) * shown
    states = states + token_vectors[2] * masked + token_vectors[1] * is_class

    kept = []
    for index in range(layers):
        states, saved = layer_forward(states, full[index], layer_vectors[index], biases[index])
        kept.append(saved)

    flat_positions = (positions - 1 + TOK * jnp.arange(count, dtype=jnp.int32)[:, None]).reshape(-1)
    flat_positions = jnp.pad(flat_positions, (0, row_count - picked), constant_values=-1)
    select = (flat_positions[:, None] == jnp.arange(tokens, dtype=jnp.int32)[None, :]).astype(BF)
    rows = dot(select, layer_norm(states, token_vectors[3], token_vectors[4])).astype(BF)

    all_rows = gather_rows(rows)
    flat_codes = jnp.pad(codes.reshape(-1), (0, row_count - picked), constant_values=-1)
    all_codes = gather_rows(flat_codes)
    head_low = head_weight.astype(BF)
    logits = dot(all_rows, head_low) + vocab_bias
    local_max = jnp.max(logits, axis=1)
    local_sum = jnp.sum(jnp.exp(logits - local_max[:, None]), axis=1)
    hits = all_codes[:, None] == vocab_ids[None, :]
    local_target = jnp.sum(jnp.where(hits, logits, 0.0), axis=1)
    stats = gather_stats(jnp.stack([local_max, local_sum, local_target]))
    top = jnp.max(stats[:, 0], axis=0)
    total = jnp.sum(stats[:, 1] * jnp.exp(stats[:, 0] - top), axis=0)
    target = jnp.sum(stats[:, 2], axis=0)
    log_total = top + jnp.log(total)
    valid = all_codes >= 0
    row_loss = jnp.where(valid, log_total - target, 0.0)
    loss_sum = jnp.sum(lax.dynamic_slice_in_dim(row_loss, place * row_count, row_count))
    logit_grads = jnp.exp(logits - log_total[:, None]) - hits.astype(F32)
    logit_grads = jnp.where(valid[:, None], logit_grads, 0.0)
    rounded = logit_grads.astype(BF)
    grad_head = dot(all_rows, rounded, TN)
    grad_vocab = jnp.sum(logit_grads, axis=0)
    row_grads = scatter_rows(dot(rounded, head_low, NT).astype(BF))

    high, middle, unused = three_parts(row_grads)
    dnormed = dot(select, high, TN) + dot(select, middle, TN)
    back, dgain, dbias = layer_norm_back(states, token_vectors[3], dnormed)
    deltas = [None] * layers
    grad_layers = [None] * layers
    for index in reversed(range(layers)):
        back, deltas[index], grad_layers[index] = layer_back(
            back, kept[index], full[index], layer_vectors[index]
        )
    dpatch = (back * shown).astype(BF)
    grad_token = jnp.stack(
        [
            jnp.sum(dpatch.astype(F32), axis=0),
            jnp.sum(back * is_class, axis=0),
            jnp.sum(back * masked, axis=0),
            dgain,
            dbias,
        ]
    )
    delta_patch = dot(dpatch, flat_patches, TN).astype(BF)
    grad_layer = jnp.stack(grad_layers)

    reduced = reduce_weights([delta_patch] + [item for delta in deltas for item in delta])
    grad_head = lax.psum(grad_head.astype(BF), "grp").astype(F32)
    grad_vocab = lax.psum(grad_vocab, "grp")
    grad_token, grad_layer, loss_sum = lax.psum((grad_token, grad_layer, loss_sum), ("grp", "fsdp"))
    sharded_squares = jnp.zeros((), F32)
    for grad in reduced + [grad_head, grad_vocab]:
        sharded_squares = sharded_squares + jnp.sum(grad * grad)
    replicated_squares = jnp.sum(grad_token * grad_token) + jnp.sum(grad_layer * grad_layer)
    squares = lax.psum(sharded_squares + replicated_squares / lax.axis_size("fsdp"), "fsdp")
    clip_norm = jnp.sqrt(squares)
    clip_scale = jnp.minimum(1.0, clip_level / (clip_norm + 1e-06))
    updates = [
        adam_step(
            patch_weight,
            reduced[0].T * clip_scale,
            first_patch,
            second_patch,
            weight_decay,
            matrix_rate,
        ),
        adam_step(
            head_weight, grad_head * clip_scale, first_head, second_head, weight_decay, matrix_rate
        ),
        adam_step(vocab_bias, grad_vocab * clip_scale, first_vocab, second_vocab, 0.0, vector_rate),
        adam_step(
            token_vectors, grad_token * clip_scale, first_token, second_token, 0.0, vector_rate
        ),
    ]
    matrices = [
        (qkv_weight, first_qkv, second_qkv),
        (out_weight, first_out, second_out),
        (up_weight, first_up, second_up),
        (down_weight, first_down, second_down),
    ]
    for kind in range(4):
        weight_all, moment_all, square_all = matrices[kind]
        results = []
        for index in range(layers):
            basis = bases[4 * index + kind]
            grad = reduced[1 + 4 * index + kind]
            if kind < 3:
                turned = product(basis, grad, (((0,), (1,)), ((), ())))
            else:
                turned = product(grad, basis)
            update, moment, square = adam_parts(
                turned * clip_scale, moment_all[index], square_all[index]
            )
            update = product(basis, update) if kind < 3 else product(update, basis, NT)
            weight = weight_all[index]
            results.append(
                (weight - matrix_rate * (update + weight_decay * weight), moment, square)
            )
        updates.append(
            tuple((jnp.stack([result[member] for result in results]) for member in range(3)))
        )
    updates.append(
        adam_step(
            layer_vectors, grad_layer * clip_scale, first_layer, second_layer, 0.0, vector_rate
        )
    )
    return (
        loss_sum,
        clip_norm,
        *[entry[0] for entry in updates],
        *[entry[1] for entry in updates],
        *[entry[2] for entry in updates],
    )


def solution(mesh):
    weights = (
        P(None, "fsdp"),
        P(None, "fsdp"),
        P("fsdp"),
        P(),
        P(None, None, "fsdp"),
        P(None, None, "fsdp"),
        P(None, None, "fsdp"),
        P(None, "fsdp", None),
        P(),
    )
    placed = (
        P(("grp", "fsdp"), None, None),
        P(("grp", "fsdp"), None),
        P(("grp", "fsdp"), None),
        P(),
        P(),
        *weights,
        *weights,
        *weights,
    )
    return jax.shard_map(
        body,
        mesh=mesh,
        in_specs=placed,
        out_specs=(P(), P(), *weights, *weights, *weights),
        check_vma=False,
    )
```

time: 3370 us -> 2070 us (0.61)
  waiting for transfers between devices: 1890 us -> 1420 us
  local copies, waits for them, and re-layouts: 469 us -> 54.3 us
  matrix products: 454 us -> 258 us
  other arithmetic: 218 us -> 89.7 us
  blocking collectives: 261 us -> 135 us
  Pallas kernels: 0 us -> 73.5 us
    unnamed x42 -> x22, waiting for transfers between devices: 369 us -> 2.21 us
    psum x2 -> x1, waiting for transfers between devices: 333 us -> 107 us  [reduce_weights(): return [lax.psum(part, 'grp').astype(F32) for part in scattered]]
    reshape x28 -> x5, local copies, waits for them, and re-layouts: 203 us -> 0.42 us  [the longest x2 0.18 us: layer_back(): dtable.reshape(-1)]
    dot_general x100 -> x48, matrix products: 454 us -> 258 us  [the longest x32 212 us: dot(): return lax.dot_general(a, b, dims, preferred_element_type=F32)]
    unnamed x3 -> x1, blocking collectives: 193 us -> 35.3 us
    unnamed x943 -> x303, local copies, waits for them, and re-layouts: 131 us -> 32.6 us
    all_gather x11 -> x10, waiting for transfers between devices: 413 us -> 503 us  [the longest x9 473 us: gather_weights(): lax.all_gather(shard, 'fsdp', axis=0, tiled=True)]
    pallas_call x0 -> x8, Pallas kernels: none -> 73.5 us  [the longest x2 42.2 us: attend_back(): pl.pallas_call(attend_back_kernel, grid=(count,), out_shape=(jax.ShapeDty...]
  transfers between devices with their start and end apart: 36 -> 22, of which waited for: 26 -> 21; matrix products, arithmetic and copies ran while one was open for 23% -> 9% of each run, Pallas kernels for 0% -> 2%
where the time goes in v1:
time: 2070 us; the launch traced here: 2060 us
  waiting for transfers between devices  1420 us (69%)
  matrix products  258 us (12%)
  blocking collectives  135 us (7%)
  other arithmetic  89.7 us (4%)
  Pallas kernels  73.5 us (4%)
  local copies, waits for them, and re-layouts  54.3 us (3%)
  between operations  27.7 us (1%)
    reduce_scatter x9, waiting for transfers between devices, reduce_weights(): lax.psum_scatter(grad, 'fsdp', scatter_dimension=0, tiled=True)  666 us
    all_gather x9, waiting for transfers between devices, gather_weights(): lax.all_gather(shard, 'fsdp', axis=0, tiled=True)  473 us
    dot_general x32, matrix products, dot(): return lax.dot_general(a, b, dims, preferred_element_type=F32)  212 us
    psum x1, waiting for transfers between devices, reduce_weights(): return [lax.psum(part, 'grp').astype(F32) for part in scattered]  107 us
    reduce_scatter x1, waiting for transfers between devices, scatter_rows(): lax.psum_scatter(grads, 'fsdp', scatter_dimension=0, tiled=True).astype(F32)  80.5 us
    psum x1, waiting for transfers between devices, body(): lax.psum((grad_token, grad_layer, loss_sum), ('grp', 'fsdp'))  64.6 us
    dot_general x16, matrix products, product(): lax.dot_general(left_side, right_side, dims, precision=lax.Precision.HIGH...  45.5 us
    pallas_call x2, Pallas kernels, attend_back(): pl.pallas_call(attend_back_kernel, grid=(count,), out_shape=(jax.ShapeDty...  42.2 us
  transfers between devices with their start and end apart: 22, of which 21 were waited for; matrix products, arithmetic and copies ran while one was open for 9% of the time, Pallas kernels for 2%

profile of v1, /device:TPU:0, one launch (start us, length us, event | category | flops | bytes accessed | tf_op | source)
XLA Modules:
  0.0 2063.8 jit_solution(18101694481067225287)
XLA Ops:
  33.8 20.8 %all-gather.13.cloned.1.call-done = bf16[768,768]{1,0:T(8,128)(2,1)} async-done(((bf16[96,768]{1,0:T(8,128)(2,1)}), bf16[768,768]{1,0:T(8,128)(2,1)}) %all-gather.13.cloned.1.call-update) | async-done | bytes 1179664 | tf_op jit(solution)/shard_map/all_gather | solution.py:348
  59.7 61.6 %all-gather.15.cloned.1.call-done = bf16[2304,768]{1,0:T(8,128)(2,1)} async-done(((bf16[288,768]{1,0:T(8,128)(2,1)}), bf16[2304,768]{1,0:T(8,128)(2,1)}) %all-gather.15.cloned.1.call-update) | async-done | bytes 3538960 | tf_op jit(solution)/shard_map/all_gather | solution.py:348
  121.4 8.1 add_convert_fusion.1.qkv_ref
  129.5 9.6 shard_map.519
  140.1 23.6 %all-gather.17.cloned.1.call-done = bf16[768,768]{1,0:T(8,128)(2,1)} async-done(((bf16[96,768]{1,0:T(8,128)(2,1)}), bf16[768,768]{1,0:T(8,128)(2,1)}) %all-gather.17.cloned.1.call-update) | async-done | bytes 1179664 | tf_op jit(solution)/shard_map/all_gather | solution.py:348
  170.9 74.2 %all-gather.19.cloned.1.call-done = bf16[3072,768]{1,0:T(8,128)(2,1)} async-done(((bf16[384,768]{1,0:T(8,128)(2,1)}), bf16[3072,768]{1,0:T(8,128)(2,1)}) %all-gather.19.cloned.1.call-update) | async-done | bytes 4718608 | tf_op jit(solution)/shard_map/all_gather | solution.py:348
  245.0 10.6 multiply_convert_fusion.3
  255.7 70.0 %all-gather.21.cloned.1.call-done = bf16[3072,768]{1,0:T(8,128)(2,1)} async-done(((bf16[384,768]{1,0:T(8,128)(2,1)}), bf16[3072,768]{1,0:T(8,128)(2,1)}) %all-gather.21.cloned.1.call-update) | async-done | bytes 4718608 | tf_op jit(solution)/shard_map/all_gather | solution.py:348
  325.7 10.4 fusion.420
  338.0 53.7 %all-gather.23.cloned.1.call-done = bf16[2304,768]{1,0:T(8,128)(2,1)} async-done(((bf16[288,768]{1,0:T(8,128)(2,1)}), bf16[2304,768]{1,0:T(8,128)(2,1)}) %all-gather.23.cloned.1.call-update) | async-done | bytes 3538960 | tf_op jit(solution)/shard_map/all_gather | solution.py:348
  391.6 8.0 add_convert_fusion.qkv_ref
  399.7 9.2 shard_map.521
  409.9 24.0 %all-gather.25.cloned.1.call-done = bf16[768,768]{1,0:T(8,128)(2,1)} async-done(((bf16[96,768]{1,0:T(8,128)(2,1)}), bf16[768,768]{1,0:T(8,128)(2,1)}) %all-gather.25.cloned.1.call-update) | async-done | bytes 1179664 | tf_op jit(solution)/shard_map/all_gather | solution.py:348
  439.7 75.7 %all-gather.27.cloned.1.call-done = bf16[3072,768]{1,0:T(8,128)(2,1)} async-done(((bf16[384,768]{1,0:T(8,128)(2,1)}), bf16[3072,768]{1,0:T(8,128)(2,1)}) %all-gather.27.cloned.1.call-update) | async-done | bytes 4718608 | tf_op jit(solution)/shard_map/all_gather | solution.py:348
  515.4 11.3 multiply_convert_fusion.2
  526.7 69.5 %all-gather.29.cloned.1.call-done = bf16[3072,768]{1,0:T(8,128)(2,1)} async-done(((bf16[384,768]{1,0:T(8,128)(2,1)}), bf16[3072,768]{1,0:T(8,128)(2,1)}) %all-gather.29.cloned.1.call-update) | async-done | bytes 4718608 | tf_op jit(solution)/shard_map/all_gather | solution.py:348
  596.2 9.6 fusion.418
  610.7 35.3 %all-reduce.5 = s32[2432]{0:T(1024)S(1)} all-reduce(s32[2432]{0:T(1024)S(1)} %pad_dynamic-update-slice_fusion), channel_id=1, replica_groups=mesh['grp'=4,'fsdp'=8] {'fsdp'}, use_global_device_ids=true, to_apply=%add.5 | all-reduce | flops 2432 | bytes 19456
  646.0 29.4 %all-gather.31.cloned.1.call-done = bf16[2432,768]{1,0:T(8,128)(2,1)} async-done(((bf16[304,768]{1,0:T(8,128)(2,1)}), bf16[2432,768]{1,0:T(8,128)(2,1)}) %all-gather.31.cloned.1.call-update) | async-done | bytes 3735568 | tf_op jit(solution)/shard_map/all_gather | solution.py:352
  675.5 7.7 add_reduce_fusion
  687.2 31.0 %all-gather.1 = f32[8,3,2432]{2,1,0:T(4,128)S(1)} all-gather(f32[1,3,2432]{2,1,0:T(4,128)S(1)} %maximum_bitcast_fusion), channel_id=2, replica_groups=mesh['grp'=4,'fsdp'=8] {'fsdp'}, dimensions={0}, use_global_device_ids=true | all-gather | bytes 262656 | tf_op jit(solution)/shard_map/all_gather | solution.py:356
  731.8 80.5 %reduce-scatter.11.cloned.1.call-done = bf16[304,768]{1,0:T(8,128)(2,1)} async-done(((bf16[2432,768]{1,0:T(8,128)(2,1)}), bf16[304,768]{1,0:T(8,128)(2,1)}) %reduce-scatter.11.cloned.1.call-update) | async-done | bytes 466960 | tf_op jit(solution)/shard_map/reduce_scatter | solution.py:360
  819.9 10.7 convert_reduce_fusion
  839.1 21.1 %shard_map.522 = (bf16[832,2304]{1,0:T(8,128)(2,1)}, f32[12,208,208]{2,1,0:T(8,128)S(1)}) custom-call(bf16[832,2304]{1,0:T(8,128)(2,1)} %add_convert_fusion.qkv_ref, bf16[4,12,208,208]{3,2,1,0:T(8,128)(2,1)} %get-tuple-element.39.prob_ref, bf16[832,768]{1,0:T(8,128)(2,1)S(1)} %convolution_convert_fusion.9.grad_ref), custom_call_target="tpu_custom_call" | custom-call | tf_op jit(solution)/shard_map/pallas_call | solution.py:216
  868.8 9.0 convert_reduce_fusion.1
  886.5 21.1 %shard_map.523 = (bf16[832,2304]{1,0:T(8,128)(2,1)}, f32[12,208,208]{2,1,0:T(8,128)S(1)}) custom-call(bf16[832,2304]{1,0:T(8,128)(2,1)} %add_convert_fusion.1.qkv_ref, bf16[4,12,208,208]{3,2,1,0:T(8,128)(2,1)} %get-tuple-element.41.prob_ref, bf16[832,768]{1,0:T(8,128)(2,1)S(1)} %convolution_convert_fusion.8.grad_ref), custom_call_target="tpu_custom_call" | custom-call | tf_op jit(solution)/shard_map/pallas_call | solution.py:216
  907.6 7.6 multiply_reduce_fusion.7
  929.1 8.8 convolution_convert_fusion.1
  938.5 8.9 convolution_convert_fusion
  948.1 9.7 convolution_convert_fusion.5
  958.0 8.9 convolution_convert_fusion.4
  967.6 9.8 convolution_convert_fusion.3
  977.5 8.8 convolution_convert_fusion.2
  1001.3 9.0 convolution_convert_fusion.7
  1010.3 40.9 %reduce-scatter.17.cloned.1.call-done = bf16[96,768]{1,0:T(8,128)(2,1)} async-done(((bf16[768,768]{1,0:T(8,128)(2,1)}), bf16[96,768]{1,0:T(8,128)(2,1)}) %reduce-scatter.17.cloned.1.call-update) | async-done | bytes 147472 | tf_op jit(solution)/shard_map/reduce_scatter | solution.py:365
  1051.1 67.0 %reduce-scatter.25.cloned.1.call-done = bf16[96,768]{1,0:T(8,128)(2,1)} async-done(((bf16[768,768]{1,0:T(8,128)(2,1)}), bf16[96,768]{1,0:T(8,128)(2,1)}) %reduce-scatter.25.cloned.1.call-update) | async-done | bytes 147472 | tf_op jit(solution)/shard_map/reduce_scatter | solution.py:365
  1118.2 81.7 %reduce-scatter.15.cloned.1.call-done = bf16[288,768]{1,0:T(8,128)(2,1)} async-done(((bf16[2304,768]{1,0:T(8,128)(2,1)}), bf16[288,768]{1,0:T(8,128)(2,1)}) %reduce-scatter.15.cloned.1.call-update) | async-done | bytes 442384 | tf_op jit(solution)/shard_map/reduce_scatter | solution.py:365
  1199.9 82.2 %reduce-scatter.23.cloned.1.call-done = bf16[288,768]{1,0:T(8,128)(2,1)} async-done(((bf16[2304,768]{1,0:T(8,128)(2,1)}), bf16[288,768]{1,0:T(8,128)(2,1)}) %reduce-scatter.23.cloned.1.call-update) | async-done | bytes 442384 | tf_op jit(solution)/shard_map/reduce_scatter | solution.py:365
  1282.1 98.9 %reduce-scatter.19.cloned.1.call-done = bf16[384,768]{1,0:T(8,128)(2,1)} async-done(((bf16[3072,768]{1,0:T(8,128)(2,1)}), bf16[384,768]{1,0:T(8,128)(2,1)}) %reduce-scatter.19.cloned.1.call-update) | async-done | bytes 589840 | tf_op jit(solution)/shard_map/reduce_scatter | solution.py:365
  1381.0 98.5 %reduce-scatter.21.cloned.1.call-done = bf16[384,768]{1,0:T(8,128)(2,1)} async-done(((bf16[3072,768]{1,0:T(8,128)(2,1)}), bf16[384,768]{1,0:T(8,128)(2,1)}) %reduce-scatter.21.cloned.1.call-update) | async-done | bytes 589840 | tf_op jit(solution)/shard_map/reduce_scatter | solution.py:365
  1479.5 98.7 %reduce-scatter.27.cloned.1.call-done = bf16[384,768]{1,0:T(8,128)(2,1)} async-done(((bf16[3072,768]{1,0:T(8,128)(2,1)}), bf16[384,768]{1,0:T(8,128)(2,1)}) %reduce-scatter.27.cloned.1.call-update) | async-done | bytes 589840 | tf_op jit(solution)/shard_map/reduce_scatter | solution.py:365
  1578.2 98.5 %reduce-scatter.29.cloned.1.call-done = bf16[384,768]{1,0:T(8,128)(2,1)} async-done(((bf16[3072,768]{1,0:T(8,128)(2,1)}), bf16[384,768]{1,0:T(8,128)(2,1)}) %reduce-scatter.29.cloned.1.call-update) | async-done | bytes 589840 | tf_op jit(solution)/shard_map/reduce_scatter | solution.py:365
  1686.1 7.1 psum.116
  1698.2 40.1 %all-reduce.6 = (f32[]{:T(128)}, f32[5,768]{1,0:T(8,128)}) all-reduce(f32[]{:T(128)} %fusion.352, f32[5,768]{1,0:T(8,128)} %stack.156), channel_id=1, replica_groups=mesh['grp'=4,'fsdp'=8] {'grp','fsdp'}, use_global_device_ids=true, to_apply=%region_18.19 | all-reduce | flops 3841 | bytes 30728 | tf_op jit(solution)/shard_map/psum | solution.py:496
  1739.7 64.6 %all-reduce.11.cloned.1.call-done = f32[2,19536]{1,0:T(2,128)} async-done(((f32[2,19536]{1,0:T(2,128)}), f32[2,19536]{1,0:T(2,128)}) %all-reduce.11.cloned.1.call-update) | async-done | bytes 156304 | tf_op jit(solution)/shard_map/psum | solution.py:496
  1807.2 107.3 %all-reduce.13.cloned.1.call-done = (bf16[96,768]{1,0:T(8,128)(2,1)}, bf16[288,768]{1,0:T(8,128)(2,1)}, bf16[96,768]{1,0:T(8,128)(2,1)}, bf16[384,768]{1,0:T(8,1...) async-done(((bf16[96,768]{1,0:T(8,128)(2,1)}, ...) | async-done | bytes 5259280 | tf_op jit(solution)/shard_map/psum | solution.py:367
  1941.2 21.8 %psum.119 = f32[]{:T(128)} all-reduce(f32[]{:T(128)S(6)} %add.611), channel_id=1, replica_groups=mesh['grp'=4,'fsdp'=8] {'fsdp'}, use_global_device_ids=true, to_apply=%region_91.92 | all-reduce | flops 1 | bytes 8 | tf_op jit(solution)/shard_map/psum | solution.py:501
  2032.9 7.1 multiply_subtract_fusion
  (518 shorter events, 254.3 us)
Async XLA Ops:
  7.2 47.4 %all-gather.13.cloned.1.call-start = ((), (), s32[]{:S(2)}) async-start(), calls=%async_computation.10 | async-start | bytes 1327104 | tf_op jit(solution)/shard_map/all_gather | solution.py:348
  9.0 112.4 %all-gather.15.cloned.1.call-start = ((), (), s32[]{:S(2)}) async-start(), calls=%async_computation.11 | async-start | bytes 3981312 | tf_op jit(solution)/shard_map/all_gather | solution.py:348
  11.5 152.2 %all-gather.17.cloned.1.call-start = ((), (), s32[]{:S(2)}) async-start(), calls=%async_computation.12 | async-start | bytes 1327104 | tf_op jit(solution)/shard_map/all_gather | solution.py:348
  12.3 232.7 %all-gather.19.cloned.1.call-start = ((), (), s32[]{:S(2)}) async-start(), calls=%async_computation.13 | async-start | bytes 5308416 | tf_op jit(solution)/shard_map/all_gather | solution.py:348
  15.5 310.1 %all-gather.21.cloned.1.call-start = ((), (), s32[]{:S(2)}) async-start(), calls=%async_computation.14 | async-start | bytes 5308416 | tf_op jit(solution)/shard_map/all_gather | solution.py:348
  18.4 373.3 %all-gather.23.cloned.1.call-start = ((), (), s32[]{:S(2)}) async-start(), calls=%async_computation.15 | async-start | bytes 3981312 | tf_op jit(solution)/shard_map/all_gather | solution.py:348
  18.9 415.0 %all-gather.25.cloned.1.call-start = ((), (), s32[]{:S(2)}) async-start(), calls=%async_computation.16 | async-start | bytes 1327104 | tf_op jit(solution)/shard_map/all_gather | solution.py:348
  19.7 495.7 %all-gather.27.cloned.1.call-start = ((), (), s32[]{:S(2)}) async-start(), calls=%async_computation.17 | async-start | bytes 5308416 | tf_op jit(solution)/shard_map/all_gather | solution.py:348
  21.1 575.2 %all-gather.29.cloned.1.call-start = ((), (), s32[]{:S(2)}) async-start(), calls=%async_computation.18 | async-start | bytes 5308416 | tf_op jit(solution)/shard_map/all_gather | solution.py:348
  21.8 653.7 %all-gather.31.cloned.1.call-start = ((), (), s32[]{:S(2)}) async-start(), calls=%async_computation.19 | async-start | bytes 4202496 | tf_op jit(solution)/shard_map/all_gather | solution.py:352
  22.1 99.3 %copy-start.92 = (f32[768]{0:T(1024)}, f32[768]{0:T(1024)S(1)}, u32[]{:S(2)}) copy-start(f32[768]{0:T(1024)S(1)} %get-tuple-element.205) | copy-start | bytes 9220
  22.1 99.3 %copy-start.113 = (f32[768]{0:T(1024)}, f32[768]{0:T(1024)S(1)}, u32[]{:S(2)}) copy-start(f32[768]{0:T(1024)S(1)} %get-tuple-element.204) | copy-start | bytes 9220
  22.1 141.6 %copy-start.80 = (f32[768]{0:T(1024)}, f32[768]{0:T(1024)S(1)}, u32[]{:S(2)}) copy-start(f32[768]{0:T(1024)S(1)} %get-tuple-element.201) | copy-start | bytes 9220
  22.1 141.6 %copy-start.88 = (f32[768]{0:T(1024)}, f32[768]{0:T(1024)S(1)}, u32[]{:S(2)}) copy-start(f32[768]{0:T(1024)S(1)} %get-tuple-element.206) | copy-start | bytes 9220
  22.1 222.9 %copy-start.109 = (f32[768]{0:T(1024)}, f32[768]{0:T(1024)S(1)}, u32[]{:S(2)}) copy-start(f32[768]{0:T(1024)S(1)} %get-tuple-element.198) | copy-start | bytes 9220
  22.1 369.5 %copy-start.111 = (f32[768]{0:T(1024)}, f32[768]{0:T(1024)S(1)}, u32[]{:S(2)}) copy-start(f32[768]{0:T(1024)S(1)} %get-tuple-element.194) | copy-start | bytes 9220
  22.1 493.3 %copy-start.107 = (f32[768]{0:T(1024)}, f32[768]{0:T(1024)S(1)}, u32[]{:S(2)}) copy-start(f32[768]{0:T(1024)S(1)} %get-tuple-element.189) | copy-start | bytes 9220
  22.5 32.2 %copy-start.96 = (f32[832]{0:T(1024)}, f32[832]{0:T(1024)S(1)}, u32[]{:S(2)}) copy-start(f32[832]{0:T(1024)S(1)} %reshape.323) | copy-start | bytes 9988
  23.0 31.7 %copy-start.86 = (f32[832]{0:T(1024)}, f32[832]{0:T(1024)S(1)}, u32[]{:S(2)}) copy-start(f32[832]{0:T(1024)S(1)} %reshape.318) | copy-start | bytes 9988
  31.3 26.4 %copy-start.100 = (f32[832]{0:T(1024)}, f32[832]{0:T(1024)S(1)}, u32[]{:S(2)}) copy-start(f32[832]{0:T(1024)S(1)} %subtract_select_fusion) | copy-start | bytes 9988
  57.8 71.7 %copy-start.84 = (f32[832]{0:T(1024)}, f32[832]{0:T(1024)S(1)}, u32[]{:S(2)}) copy-start(f32[832]{0:T(1024)S(1)} %broadcast_multiply_fusion.14) | copy-start | bytes 9988
  59.7 69.8 %copy-start.98 = (f32[832]{0:T(1024)}, f32[832]{0:T(1024)S(1)}, u32[]{:S(2)}) copy-start(f32[832]{0:T(1024)S(1)} %add_rsqrt_fusion.4) | copy-start | bytes 9988
  439.2 396.1 %copy-start.8 = (f32[832,768]{1,0:T(8,128)}, f32[832,768]{1,0:T(8,128)S(1)}, u32[]{:S(2)}) copy-start(f32[832,768]{1,0:T(8,128)S(1)} %get-tuple-element.261) | copy-start | bytes 7667716
  607.3 68.2 %copy-start.82 = (f32[1024]{0:T(1024)S(1)}, f32[1024]{0:T(1024)}, u32[]{:S(2)}) copy-start(f32[1024]{0:T(1024)} %param.38) | copy-start | bytes 12292
  609.1 203.1 %reduce-scatter.11.cloned.1.call-start = ((), (), s32[]{:S(2)}) async-start(), calls=%async_computation.20 | async-start | bytes 4202496 | tf_op jit(solution)/shard_map/reduce_scatter | solution.py:360
  646.0 73.0 %copy-start.104 = (pred[2432]{0:T(1024)(128)(4,1)}, pred[2432]{0:T(1024)(128)(4,1)S(1)}, u32[]{:S(2)}) copy-start(pred[2432]{0:T(1024)(128)(4,1)S(1)} %broadcast_compare_fusion) | copy-start | bytes 7300
  731.7 278.5 %reduce-scatter.13.cloned.1.call-start = ((), (), s32[]{:S(2)}) async-start(), calls=%async_computation.21 | async-start | bytes 1327104 | tf_op jit(solution)/shard_map/reduce_scatter | solution.py:365
  839.1 21.1 %copy-start.10 = (f32[832,768]{1,0:T(8,128)S(1)}, f32[832,768]{1,0:T(8,128)}, u32[]{:S(2)}) copy-start(f32[832,768]{1,0:T(8,128)} %copy-done.9) | copy-start | bytes 7667716
  886.4 21.1 %copy-start.12 = (f32[832,768]{1,0:T(8,128)S(1)}, f32[832,768]{1,0:T(8,128)}, u32[]{:S(2)}) copy-start(f32[832,768]{1,0:T(8,128)} %copy-done.11) | copy-start | bytes 7667716
  886.4 21.1 %copy-start.85 = (f32[832]{0:T(1024)S(1)}, f32[832]{0:T(1024)}, u32[]{:S(2)}) copy-start(f32[832]{0:T(1024)} %copy-done.84) | copy-start | bytes 9988
  886.4 21.1 %copy-start.93 = (f32[768]{0:T(1024)S(1)}, f32[768]{0:T(1024)}, u32[]{:S(2)}) copy-start(f32[768]{0:T(1024)} %copy-done.92) | copy-start | bytes 9220
  886.5 21.1 %copy-start.99 = (f32[832]{0:T(1024)S(1)}, f32[832]{0:T(1024)}, u32[]{:S(2)}) copy-start(f32[832]{0:T(1024)} %copy-done.98) | copy-start | bytes 9988
  920.2 131.0 %reduce-scatter.17.cloned.1.call-start = ((), (), s32[]{:S(2)}) async-start(), calls=%async_computation.23 | async-start | bytes 1327104 | tf_op jit(solution)/shard_map/reduce_scatter | solution.py:365
  924.4 193.8 %reduce-scatter.25.cloned.1.call-start = ((), (), s32[]{:S(2)}) async-start(), calls=%async_computation.27 | async-start | bytes 1327104 | tf_op jit(solution)/shard_map/reduce_scatter | solution.py:365
  928.6 271.2 %reduce-scatter.15.cloned.1.call-start = ((), (), s32[]{:S(2)}) async-start(), calls=%async_computation.22 | async-start | bytes 3981312 | tf_op jit(solution)/shard_map/reduce_scatter | solution.py:365
  937.9 344.2 %reduce-scatter.23.cloned.1.call-start = ((), (), s32[]{:S(2)}) async-start(), calls=%async_computation.26 | async-start | bytes 3981312 | tf_op jit(solution)/shard_map/reduce_scatter | solution.py:365
  947.4 433.6 %reduce-scatter.19.cloned.1.call-start = ((), (), s32[]{:S(2)}) async-start(), calls=%async_computation.24 | async-start | bytes 5308416 | tf_op jit(solution)/shard_map/reduce_scatter | solution.py:365
  957.8 521.7 %reduce-scatter.21.cloned.1.call-start = ((), (), s32[]{:S(2)}) async-start(), calls=%async_computation.25 | async-start | bytes 5308416 | tf_op jit(solution)/shard_map/reduce_scatter | solution.py:365
  966.9 611.3 %reduce-scatter.27.cloned.1.call-start = ((), (), s32[]{:S(2)}) async-start(), calls=%async_computation.28 | async-start | bytes 5308416 | tf_op jit(solution)/shard_map/reduce_scatter | solution.py:365
  977.4 699.3 %reduce-scatter.29.cloned.1.call-start = ((), (), s32[]{:S(2)}) async-start(), calls=%async_computation.29 | async-start | bytes 5308416 | tf_op jit(solution)/shard_map/reduce_scatter | solution.py:365
  986.3 817.9 %all-reduce.11.cloned.1.call-start = ((), (), s32[]{:S(2)}) async-start(), calls=%async_computation.30 | async-start | bytes 313344 | tf_op jit(solution)/shard_map/psum | solution.py:496
  1000.8 913.7 %all-reduce.13.cloned.1.call-start = ((), (), s32[]{:S(2)}) async-start(), calls=%async_computation.31 | async-start | bytes 10518528 | tf_op jit(solution)/shard_map/psum | solution.py:367
  1682.7 13.6 copy-start.94
  1914.5 14.5 copy-start.36
  1914.5 15.4 copy-start.17
  1963.8 26.9 %slice-start = ((s8[18874368]{0:T(1024)(128)(4,1)}), s8[4194304]{0:T(1024)(128)(4,1)S(1)}, s32[]{:S(2)}) async-start(s8[18874368]{0:T(1024)(128)(4,1)} %bitcast.540), calls=%async_computation.32 | async-start | bytes 8388608
  1969.4 21.2 %slice-start.1 = ((s8[18874368]{0:T(1024)(128)(4,1)}), s8[4194304]{0:T(1024)(128)(4,1)S(1)}, s32[]{:S(2)}) async-start(s8[18874368]{0:T(1024)(128)(4,1)} %bitcast.540), calls=%async_computation.33 | async-start | bytes 8388608
  1974.1 16.5 slice-start.2
  (108 other events, 460.3 us)
Sparse Core Ops, SparseCore 0:
  10.8 43.7 all-gather.12
  57.4 63.9 all-gather.14
  124.1 39.5 all-gather.16
  166.3 78.6 all-gather.18
  247.6 78.0 all-gather.20
  328.3 63.3 all-gather.22
  394.4 39.5 all-gather.24
  436.7 78.6 all-gather.26
  518.2 78.0 all-gather.28
  609.3 66.1 all-gather.30
  731.9 80.3 reduce-scatter.10
  920.3 63.7 reduce-scatter.12
  988.1 63.0 reduce-scatter.16
  1055.0 63.1 reduce-scatter.24
  1121.7 78.1 reduce-scatter.14
  1203.3 78.6 reduce-scatter.22
  1285.6 95.3 reduce-scatter.18
  1384.5 94.9 reduce-scatter.20
  1483.1 94.9 reduce-scatter.26
  1581.6 94.9 reduce-scatter.28
  1682.8 121.3 all-reduce.10
  1807.9 106.5 all-reduce.12
